TPU v7x, 512 devices: a whole 4x4x16 slice. The times are simulated.
512 devices in a mesh: replica: 8 (over x, core), fsdp: 16 (over z), owner: 4 (over y).
Axes of the slice: x: 4, y: 4, z: 16, core: 2. Of those that a mesh axis runs over, the one named last changes fastest.
Arguments:
- replica_grads: bfloat16 [8, 2, 4, 1024, 4096], P('replica', None, None, 'fsdp', 'owner'), may hold values from -0.15625 to 0.15625
- owner_table: int32 [4, 8, 1], replicated, may hold values from 0 to 7; in each aligned block of 8 rows (0 to 7, 8 to 15, ..., all dimensions but the last counted through in order) at most 2 rows name the same one
- stats_left: float32 [8, 4, 2, 1024, 1024], P('replica', 'owner', None, 'fsdp'), may hold values from -6 to 6
- stats_right: float32 [8, 4, 2, 1024, 1024], P('replica', 'owner', None, 'fsdp'), may hold values from -6 to 6
- left_root: bfloat16 [8, 4, 2, 1024, 1024], P('replica', 'owner', None, 'fsdp'), may hold values from -2.5 to 2.5
- right_root: bfloat16 [8, 4, 2, 1024, 1024], P('replica', 'owner', None, 'fsdp'), may hold values from -2.5 to 2.5
Outputs:
- update: bfloat16 [2, 4, 1024, 4096], P(None, None, 'fsdp', 'owner')
- new_left: float32 [8, 4, 2, 1024, 1024], P('replica', 'owner', None, 'fsdp')
- new_right: float32 [8, 4, 2, 1024, 1024], P('replica', 'owner', None, 'fsdp')
Inputs may be any that keep to these rules, and one draw needn't show every extreme that they name: `owner_table`: in each block column no group owns more than 2 of its 8 blocks, and some group owns exactly 2.
All inputs are finite; a program needn't handle non-finite values.
Results may differ from a plain program's by a relative error of at most 0.019.
Values may be sent and summed in bfloat16 or wider, within the bound.
No kernel may reach another device: no remote copies, remote signals or barrier semaphores. Data moves between devices by JAX's collectives and lax.ppermute only.
A program may use at most 64 MiB of HBM per device.

v0:
```python
import jax
import jax.numpy as jnp
from jax import lax
from jax.sharding import PartitionSpec as P


def slot_onehot(column, replicas, slot_count):
    length = column.shape[0]
    matching = column[:, None] == column[None, :]
    earlier = jnp.arange(length)[None, :] < jnp.arange(length)[:, None]
    slot_index = jnp.sum(jnp.logical_and(matching, earlier).astype(jnp.int32), axis=1)
    owners_hit = column[None, None, :] == jnp.arange(replicas, dtype=jnp.int32)[:, None, None]
    slots_hit = slot_index[None, None, :] == jnp.arange(slot_count, dtype=jnp.int32)[None, :, None]
    return jnp.logical_and(owners_hit, slots_hit).astype(jnp.float32)


def local(replica_grads, owner_table, stats_left, stats_right, left_root, right_root):
    replicas = lax.axis_size("replica")
    local_grads = replica_grads[0]
    matrices, rows_blocks, strip_rows, block_width = local_grads.shape
    tile_rows = local_grads.reshape(matrices * rows_blocks, strip_rows * block_width)
    slot_count = stats_left.shape[2]
    column = lax.dynamic_index_in_dim(
        owner_table[:, :, 0], lax.axis_index("owner"), 0, keepdims=False
    )
    onehot = slot_onehot(column, replicas, slot_count)
    flat_hot = onehot.reshape(replicas * slot_count, matrices * rows_blocks).astype(jnp.bfloat16)
    packed_wide = jnp.dot(flat_hot, tile_rows, preferred_element_type=jnp.float32)
    packed = packed_wide.astype(jnp.bfloat16).reshape(replicas, slot_count, strip_rows, block_width)
    arrived = lax.all_to_all(packed, "replica", split_axis=0, concat_axis=0, tiled=True)
    summed = jnp.sum(arrived, axis=0, dtype=jnp.float32)
    own_block = summed.astype(jnp.bfloat16)
    position = lax.axis_index("fsdp") * strip_rows
    own_left = left_root[0, 0]
    own_right = right_root[0, 0]
    whole_block = lax.all_gather(own_block, "fsdp", axis=1, tiled=True)
    left_term = jnp.einsum(
        "sik,sjk->sij", own_block, whole_block, preferred_element_type=jnp.float32
    )
    own_cols = lax.dynamic_slice_in_dim(whole_block, position, strip_rows, 2)
    right_term = jnp.einsum(
        "ski,skj->sij", own_cols, whole_block, preferred_element_type=jnp.float32
    )
    product = jnp.einsum("sik,skj->sij", own_left, whole_block, preferred_element_type=jnp.float32)
    new_left = stats_left + left_term[None, None]
    new_right = stats_right + right_term[None, None]
    product_half = product.astype(jnp.bfloat16)
    result = jnp.einsum(
        "sik,skj->sij",
        product_half,
        lax.all_gather(own_right, "fsdp", axis=1, tiled=True),
        preferred_element_type=jnp.float32,
    ).astype(jnp.bfloat16)
    everyone = lax.all_gather(result, "replica", axis=0, tiled=True)
    returned_tiles = jnp.dot(
        flat_hot.T,
        everyone.reshape(replicas * slot_count, strip_rows * block_width),
        preferred_element_type=jnp.float32,
    )
    update = returned_tiles.astype(jnp.bfloat16).reshape(
        matrices, rows_blocks, strip_rows, block_width
    )
    return (update, new_left, new_right)


def solution(mesh):
    placed = (
        P("replica", None, None, "fsdp", "owner"),
        P(),
        P("replica", "owner", None, "fsdp", None),
        P("replica", "owner", None, "fsdp", None),
        P("replica", "owner", None, "fsdp", None),
        P("replica", "owner", None, "fsdp", None),
    )
    return jax.shard_map(
        local,
        mesh=mesh,
        in_specs=placed,
        out_specs=(
            P(None, None, "fsdp", "owner"),
            P("replica", "owner", None, "fsdp", None),
            P("replica", "owner", None, "fsdp", None),
        ),
        check_vma=False,
    )
```

profile of v0, /device:TPU:1, one launch (start us, length us, event | category | flops | bytes accessed | tf_op | source)
XLA Modules:
  0.0 219.2 jit_solution(123383789081057700)
XLA Ops:
  7.2 0.0 copy-start
  7.2 0.0 all-gather.9.cloned.1.call-start
  7.2 0.7 all-gather.9.cloned.1.call-update
  7.9 0.0 all-gather.5.cloned.1.call-start
  8.0 1.8 copy.12
  9.8 0.7 dynamic-slice_bitcast_fusion
  10.4 0.2 convert_reduce_fusion
  10.7 0.7 convolution_convert_fusion
  11.3 1.2 copy.13
  12.5 35.8 %all_to_all.5 = bf16[8,2,64,1024]{3,2,1,0:T(8,128)(2,1)S(1)} all-to-all(bf16[8,2,64,1024]{3,2,1,0:T(8,128)(2,1)S(1)} %bitcast.41), channel_id=1, replica_groups=mesh['replica'=8,'fsdp'=16,'owner'=4] {'replica'}, dimensions={0} | all-to-all | bytes 4194304 | tf_op jit(solution)/shard_map/all_to_all | solution.py:30
  48.3 1.1 reduce_sum.22
  49.4 0.0 all-gather.5.cloned.1.call-update
  49.4 0.0 copy-start.3
  49.4 0.0 all-gather.7.cloned.1.call-start
  49.5 36.5 %all-gather.9.cloned.1.call-done = bf16[1,1,2,1024,1024]{4,3,2,1,0:T(8,128)(2,1)} async-done(((bf16[1,1,2,64,1024]{4,3,2,1,0:T(8,128)(2,1)}), bf16[1,1,2,1024,1024]{4,3,2,1,0:T(8,128)(2,1)}) %all-gather.9.cloned.1.call-update) | async-done | bytes 4194320 | tf_op jit(solution)/shard_map/all_gather | solution.py:51
  86.0 77.4 %all-gather.5.cloned.1.call-done = bf16[2,1024,1024]{2,1,0:T(8,128)(2,1)} async-done(((bf16[2,64,1024]{2,1,0:T(8,128)(2,1)}), bf16[2,1024,1024]{2,1,0:T(8,128)(2,1)}) %all-gather.5.cloned.1.call-update) | async-done | bytes 4194320 | tf_op jit(solution)/shard_map/all_gather | solution.py:36
  163.4 0.0 copy-done
  163.4 5.8 %fusion.4 = bf16[2,64,1024]{2,1,0:T(8,128)(2,1)} fusion(bf16[1,1,2,1024,1024]{4,3,2,1,0:T(8,128)(2,1)} %all-gather.9.cloned.1.call-done, bf16[2,1024,1024]{2,1,0:T(8,128)(2,1)} %all-gather.5.cloned.1.call-done, bf16[1,1,2,64,1024]{4,3,2,1,0:T(8,128)(2,1)S(1)} %copy-done), kind=kOutput, calls=%fused_computation.8 | convolution fusion | flops 537133056 | bytes 8912896 | tf_op jit(solution)/shard_map/sik,skj->sij/dot_general | solution.py:48
  169.2 0.0 copy-start.2
  169.2 0.0 copy-start.4
  169.2 0.0 all-gather.7.cloned.1.call-update
  169.2 0.0 copy-done.3
  169.2 0.0 copy-start.1
  169.2 4.4 %fusion.3 = f32[1,1,2,64,1024]{4,3,2,1,0:T(8,128)} fusion(f32[1,1,2,64,1024]{4,3,2,1,0:T(8,128)S(1)} %copy-done.3, bf16[2,1024,1024]{2,1,0:T(8,128)(2,1)} %all-gather.5.cloned.1.call-done, s32[]{:T(128)S(6)} %select_n.8), kind=kOutput, calls=%fused_computation.7 | convolution fusion | flops 268566528 | bytes 5767172 | tf_op jit(solution)/shard_map/ski,skj->sij/dot_general | solution.py:41
  173.6 0.0 copy-done.2
  173.6 0.0 copy-done.4
  173.6 0.0 copy-done.1
  173.6 2.2 %fusion.2 = f32[1,1,2,64,1024]{4,3,2,1,0:T(8,128)} fusion(f32[1,1,2,64,1024]{4,3,2,1,0:T(8,128)S(1)} %copy-done.4, bf16[2,64,1024]{2,1,0:T(8,128)(2,1)S(1)} %copy-done.2, bf16[2,1024,1024]{2,1,0:T(8,128)(2,1)S(1)} %copy-done.1), kind=kOutput, calls=%fused_computation.5 | convolution fusion | flops 268566528 | bytes 5505024 | tf_op jit(solution)/shard_map/sik,sjk->sij/dot_general | solution.py:37
  175.8 32.1 %all-gather.7.cloned.1.call-done = bf16[16,64,1024]{2,1,0:T(8,128)(2,1)} async-done(((bf16[2,64,1024]{2,1,0:T(8,128)(2,1)}), bf16[16,64,1024]{2,1,0:T(8,128)(2,1)}) %all-gather.7.cloned.1.call-update) | async-done | bytes 2097168 | tf_op jit(solution)/shard_map/all_gather | solution.py:54
  207.9 2.7 %copy.14 = bf16[2,8,64,1024]{3,1,2,0:T(8,128)(2,1)S(1)} copy(bf16[2,8,64,1024]{3,2,1,0:T(8,128)(2,1)} %bitcast.44) | data formatting | bytes 4194304
  210.7 0.5 convolution_convert_fusion.1
  211.2 1.5 copy.15
  (3 shorter events, 0.0 us)
Async XLA Ops:
  7.2 156.2 %copy-start = (bf16[1,1,2,64,1024]{4,3,2,1,0:T(8,128)(2,1)S(1)}, bf16[1,1,2,64,1024]{4,3,2,1,0:T(8,128)(2,1)}, u32[]{:S(2)}) copy-start(bf16[1,1,2,64,1024]{4,3,2,1,0:T(8,128)(2,1)} %param.10) | copy-start | bytes 786436
  7.2 78.8 %all-gather.9.cloned.1.call-start = ((), (), s32[]{:S(2)}) async-start(), calls=%async_computation.3 | async-start | bytes 4456448 | tf_op jit(solution)/shard_map/all_gather | solution.py:51
  7.9 155.5 %all-gather.5.cloned.1.call-start = ((), (), s32[]{:S(2)}) async-start(), calls=%async_computation.1 | async-start | bytes 4456448 | tf_op jit(solution)/shard_map/all_gather | solution.py:36
  49.4 119.8 %copy-start.3 = (f32[1,1,2,64,1024]{4,3,2,1,0:T(8,128)S(1)}, f32[1,1,2,64,1024]{4,3,2,1,0:T(8,128)}, u32[]{:S(2)}) copy-start(f32[1,1,2,64,1024]{4,3,2,1,0:T(8,128)} %param.9) | copy-start | bytes 1572868
  49.4 158.5 %all-gather.7.cloned.1.call-start = ((), (), s32[]{:S(2)}) async-start(), calls=%async_computation.2 | async-start | bytes 2359296 | tf_op jit(solution)/shard_map/all_gather | solution.py:54
  169.2 4.5 %copy-start.2 = (bf16[2,64,1024]{2,1,0:T(8,128)(2,1)S(1)}, bf16[2,64,1024]{2,1,0:T(8,128)(2,1)}, u32[]{:S(2)}) copy-start(bf16[2,64,1024]{2,1,0:T(8,128)(2,1)} %reduce_sum.22) | copy-start | bytes 786436
  169.2 4.5 %copy-start.4 = (f32[1,1,2,64,1024]{4,3,2,1,0:T(8,128)S(1)}, f32[1,1,2,64,1024]{4,3,2,1,0:T(8,128)}, u32[]{:S(2)}) copy-start(f32[1,1,2,64,1024]{4,3,2,1,0:T(8,128)} %param.8) | copy-start | bytes 1572868
  169.2 4.4 %copy-start.1 = (bf16[2,1024,1024]{2,1,0:T(8,128)(2,1)S(1)}, bf16[2,1024,1024]{2,1,0:T(8,128)(2,1)}, u32[]{:S(2)}) copy-start(bf16[2,1024,1024]{2,1,0:T(8,128)(2,1)} %all-gather.5.cloned.1.call-done) | copy-start | bytes 12582916
Sparse Core Ops, SparseCore 0:
  10.1 75.8 all-gather.8
  88.6 74.7 all-gather.4
  169.3 38.5 all-gather.6
where the time goes:
time: 219 us
  waiting for transfers between devices  147 us (67%)
  blocking collectives  35.8 us (16%)
  between operations  13.8 us (6%)
  matrix products  13.5 us (6%)
  local copies, waits for them, and re-layouts  7.94 us (4%)
    all_gather x1, waiting for transfers between devices, local(): whole_block = lax.all_gather(own_block, 'fsdp', axis=1, tiled=True)  77.4 us
    all_gather x1, waiting for transfers between devices, local(): lax.all_gather(own_right, 'fsdp', axis=1, tiled=True)  36.5 us
    all_to_all x1, blocking collectives, local(): lax.all_to_all(packed, 'replica', split_axis=0, concat_axis=0, tiled=True)  35.8 us
    all_gather x1, waiting for transfers between devices, local(): everyone = lax.all_gather(result, 'replica', axis=0, tiled=True)  32.1 us
    unnamed x14, local copies, waits for them, and re-layouts  7.28 us
    dot_general x1, matrix products, local(): jnp.einsum('sik,skj->sij', product_half, lax.all_gather(own_right, 'fsdp'...  5.75 us
    dot_general x1, matrix products, local(): jnp.einsum('ski,skj->sij', own_cols, whole_block, preferred_element_type=...  4.41 us
  transfers between devices with their start and end apart: 3, of which 3 were waited for; matrix products, arithmetic and copies ran while one was open for 6% of the time, Pallas kernels for 0%

commit v1 on v0

v1 whole, which is shorter than its diff:
```python
import jax
import jax.numpy as jnp
from jax import lax
from jax.experimental import pallas as pl
from jax.experimental.pallas import tpu as pltpu
from jax.sharding import Mesh, PartitionSpec as P

F32 = jnp.float32
BF16 = jnp.bfloat16
CORE_SWAP = ((0, 1), (1, 0))
VMEM = pl.BlockSpec(memory_space=pltpu.VMEM)
SMEM = pl.BlockSpec(memory_space=pltpu.SMEM)
PARAMS = pltpu.CompilerParams(vmem_limit_bytes=24 << 20)


def owner_and_slot(table_ref, column, q, blocks):
    owner = table_ref[column, q]
    slot = jnp.int32(0)
    for other in range(blocks):
        same = jnp.logical_and(table_ref[column, other] == owner, other < q)
        slot = slot + same.astype(jnp.int32)
    return owner, slot


def pack_kernel(table_ref, grads_ref, right_ref, left_ref, own_ref, sib_ref, own_left_ref, sib_left_ref):
    column = lax.axis_index("y")
    core = lax.axis_index("core")
    me = lax.axis_index("x") * 2 + core
    blocks = grads_ref.shape[0]
    for chip in range(own_ref.shape[0]):
        for parity, out_ref, out_left_ref in (
            (core, own_ref, own_left_ref),
            (1 - core, sib_ref, sib_left_ref),
        ):
            q = 2 * chip + parity
            out_ref[chip, 0] = grads_ref[q]
            owner, slot = owner_and_slot(table_ref, column, q, blocks)

            @pl.when(owner == me)
            def _():
                out_ref[chip, 1] = right_ref[slot]
                out_left_ref[chip] = left_ref[slot]

            @pl.when(owner != me)
            def _():
                out_ref[chip, 1] = jnp.zeros(right_ref.shape[1:], right_ref.dtype)
                out_left_ref[chip] = jnp.zeros(left_ref.shape[1:], left_ref.dtype)


def pack(table, grads, right, left, chips):
    rows, width = grads.shape[1:]
    pair = jax.ShapeDtypeStruct((chips, 2, rows, width), grads.dtype)
    single = jax.ShapeDtypeStruct((chips, rows, width), left.dtype)
    return pl.pallas_call(
        pack_kernel,
        out_shape=(pair, pair, single, single),
        in_specs=[SMEM, VMEM, VMEM, VMEM],
        out_specs=(VMEM,) * 4,
        compiler_params=PARAMS,
        name="pack",
    )(table, grads, right, left)


def unpack_kernel(table_ref, stats_left_ref, stats_right_ref, *refs):
    pieces, (update_ref, new_left_ref, new_right_ref) = refs[:-3], refs[-3:]
    column = lax.axis_index("y")
    core = lax.axis_index("core")
    x = lax.axis_index("x")
    me = x * 2 + core
    blocks = update_ref.shape[0]
    chips = blocks // 2
    new_left_ref[...] = stats_left_ref[...]
    new_right_ref[...] = stats_right_ref[...]
    for place, piece_ref in enumerate(pieces):
        chip = lax.rem(x - place // 2 + chips, chips)
        parity = core if place % 2 == 0 else 1 - core
        q = chip * 2 + parity
        update_ref[q] = piece_ref[0]
        owner, slot = owner_and_slot(table_ref, column, q, blocks)

        @pl.when(owner == me)
        def _():
            new_left_ref[slot] = stats_left_ref[slot] + piece_ref[1].astype(F32)
            new_right_ref[slot] = stats_right_ref[slot] + piece_ref[2].astype(F32)


def unpack(table, stats_left, stats_right, pieces, blocks):
    rows, width = pieces[0].shape[1:]
    stats = jax.ShapeDtypeStruct(stats_left.shape, stats_left.dtype)
    return pl.pallas_call(
        unpack_kernel,
        out_shape=(jax.ShapeDtypeStruct((blocks, rows, width), BF16), stats, stats),
        in_specs=[SMEM] + [VMEM] * (2 + len(pieces)),
        out_specs=(VMEM,) * 3,
        compiler_params=PARAMS,
        name="unpack",
    )(table, stats_left, stats_right, *pieces)


def route(own, sibling):
    swapped = lax.ppermute(sibling, "core", CORE_SWAP)
    pair = (own.astype(F32) + swapped.astype(F32)).astype(BF16)
    arrived = lax.all_to_all(pair, "x", split_axis=0, concat_axis=0, tiled=True)
    return jnp.sum(arrived, axis=0, dtype=F32).astype(BF16)


def local(replica_grads, owner_table, stats_left, stats_right, left_root, right_root):
    local_grads = replica_grads[0]
    matrices, rows_blocks, rows, width = local_grads.shape
    chips = lax.axis_size("x")
    blocks = matrices * rows_blocks
    table = owner_table[:, :, 0]
    own, sibling, own_left, sibling_left = pack(
        table, local_grads.reshape(blocks, rows, width), right_root[0, 0], left_root[0, 0], chips
    )
    strips = route(own, sibling)
    whole = lax.all_gather(strips, "z", axis=1, tiled=True)
    own_left, sibling_left, strips = lax.optimization_barrier((own_left, sibling_left, strips))
    left_strip = route(own_left, sibling_left)
    whole_block, whole_right = whole[0], whole[1]
    product = jnp.dot(left_strip, whole_block, preferred_element_type=F32).astype(BF16)
    result = jnp.dot(product, whole_right, preferred_element_type=F32).astype(BF16)
    left_term = jnp.einsum("ik,jk->ij", strips[0], whole_block, preferred_element_type=F32)
    own_cols = lax.dynamic_slice_in_dim(whole_block, lax.axis_index("z") * rows, rows, 1)
    right_term = jnp.einsum("ki,kj->ij", own_cols, whole_block, preferred_element_type=F32)
    payload = jnp.stack([result, left_term.astype(BF16), right_term.astype(BF16)])
    pieces = []
    for step in range(chips):
        piece = payload
        if step:
            piece = lax.ppermute(payload, "x", [(i, (i + step) % chips) for i in range(chips)])
        pieces += [piece, lax.ppermute(piece, "core", CORE_SWAP)]
    update, new_left, new_right = unpack(table, stats_left[0, 0], stats_right[0, 0], pieces, blocks)
    return (
        update.reshape(matrices, rows_blocks, rows, width),
        new_left[None, None],
        new_right[None, None],
    )


def solution(mesh):
    replicas, shards, columns = mesh.devices.shape
    split = Mesh(
        mesh.devices.reshape(replicas // 2, 2, shards, columns), ("x", "core", "z", "y")
    )
    replica = ("x", "core")
    owned = P(replica, "y", None, "z", None)
    return jax.shard_map(
        local,
        mesh=split,
        in_specs=(P(replica, None, None, "z", "y"), P(), owned, owned, owned, owned),
        out_specs=(P(None, None, "z", "y"), owned, owned),
        check_vma=False,
    )
```

time: 219 us -> 159 us (0.73)
  waiting for transfers between devices: 147 us -> 65.5 us
  starting transfers between devices: 0.12 us -> 44.7 us
  blocking collectives: 35.8 us -> 17.3 us
  matrix products: 13.5 us -> 6.16 us
  Pallas kernels: 0 us -> 3.01 us
  local copies, waits for them, and re-layouts: 7.94 us -> 5.41 us
    all_gather x3 -> x1, waiting for transfers between devices: 146 us -> 50.9 us  [local(): whole = lax.all_gather(strips, 'z', axis=1, tiled=True)]
    ppermute x0 -> x9, starting transfers between devices: none -> 41.2 us  [the longest x4 18.8 us: local(): pieces += [piece, lax.ppermute(piece, 'core', CORE_SWAP)]]
    all_to_all x1, blocking collectives: 35.8 us -> 17.3 us  [route(): arrived = lax.all_to_all(pair, 'x', split_axis=0, concat_axis=0, tiled=True)]
    all_to_all x0 -> x1, waiting for transfers between devices: none -> 9.19 us  [route(): arrived = lax.all_to_all(pair, 'x', split_axis=0, concat_axis=0, tiled=True)]
    dot_general x5 -> x3, matrix products: 13.5 us -> 6.16 us  [the longest x1 3.11 us: local(): jnp.dot(product, whole_right, preferred_element_type=F32).astype(BF16)]
    ppermute x0 -> x9, waiting for transfers between devices: none -> 5.45 us  [the longest x2 3.78 us: route(): swapped = lax.ppermute(sibling, 'core', CORE_SWAP)]
    all_to_all x0 -> x1, starting transfers between devices: none -> 3.47 us  [route(): arrived = lax.all_to_all(pair, 'x', split_axis=0, concat_axis=0, tiled=True)]
    unnamed x14 -> x16, local copies, waits for them, and re-layouts: 7.28 us -> 3.82 us
  transfers between devices with their start and end apart: 3 -> 11, of which waited for: 3 -> 5; matrix products, arithmetic and copies ran while one was open for 6% -> 1% of each run, Pallas kernels for 0% -> 0%
where the time goes in v1:
time: 159 us
  waiting for transfers between devices  65.5 us (41%)
  starting transfers between devices  44.7 us (28%)
  blocking collectives  17.3 us (11%)
  between operations  14.3 us (9%)
  matrix products  6.16 us (4%)
  local copies, waits for them, and re-layouts  5.41 us (3%)
  Pallas kernels  3.01 us (2%)
  other arithmetic  2.46 us (2%)
    all_gather x1, waiting for transfers between devices, local(): whole = lax.all_gather(strips, 'z', axis=1, tiled=True)  50.9 us
    ppermute x4, starting transfers between devices, local(): pieces += [piece, lax.ppermute(piece, 'core', CORE_SWAP)]  18.8 us
    all_to_all x1, blocking collectives, route(): arrived = lax.all_to_all(pair, 'x', split_axis=0, concat_axis=0, tiled=True)  17.3 us
    ppermute x2, starting transfers between devices, route(): swapped = lax.ppermute(sibling, 'core', CORE_SWAP)  11.9 us
    ppermute x3, starting transfers between devices, local(): lax.ppermute(payload, 'x', [(i, (i + step) % chips) for i in range(chips)])  10.5 us
    all_to_all x1, waiting for transfers between devices, route(): arrived = lax.all_to_all(pair, 'x', split_axis=0, concat_axis=0, tiled=True)  9.19 us
    unnamed x16, local copies, waits for them, and re-layouts  3.82 us
    ppermute x2, waiting for transfers between devices, route(): swapped = lax.ppermute(sibling, 'core', CORE_SWAP)  3.78 us
  transfers between devices with their start and end apart: 11, of which 5 were waited for; matrix products, arithmetic and copies ran while one was open for 1% of the time, Pallas kernels for 0%

profile of v1, /device:TPU:1, one launch (start us, length us, event | category | flops | bytes accessed | tf_op | source)
XLA Modules:
  0.0 158.8 jit_solution(6076811080182911105)
XLA Ops:
  7.2 0.0 all-gather.2.cloned.1.call-start
  7.2 1.2 copy-done
  8.4 0.9 copy-done.3
  9.4 0.9 copy-done.4
  10.3 0.7 copy-done.5
  11.0 0.8 pack.1
  11.9 8.8 %collective-permute-start = (bf16[4,2,64,1024]{3,2,1,0:T(8,128)(2,1)S(1)}, bf16[4,2,64,1024]{3,2,1,0:T(8,128)(2,1)S(1)}, u32[]{:S(2)}, u32[]{:S(2)}) collective-permute-start(bf16[4,2,64,1024]{3,2,1,0:T(8,128)(2,1)S(1)} %get-tuple-element.16), channel_id=1, source_target_pairs={{0,64},{64,0},{1,65},{65,1},{2,66},{66,2},{3,67},{67,3},{4,68},{68... | collective-permute-start | bytes 3145736 | tf_op jit(solution)/shard_map/ppermute | solution.py:101
  20.7 2.3 %collective-permute-done = bf16[4,2,64,1024]{3,2,1,0:T(8,128)(2,1)S(1)} collective-permute-done((bf16[4,2,64,1024]{3,2,1,0:T(8,128)(2,1)S(1)}, bf16[4,2,64,1024]{3,2,1,0:T(8,128)(2,1)S(1)}, u32[]{:S(2)}, u32[]{:S(2)}) %collective-permute-start) | collective-permute-done | bytes 1048608 | tf_op jit(solution)/shard_map/ppermute | solution.py:101
  22.9 0.4 add_convert_fusion
  23.3 17.3 %all_to_all.10 = bf16[4,2,64,1024]{3,2,1,0:T(8,128)(2,1)S(1)} all-to-all(bf16[4,2,64,1024]{3,2,1,0:T(8,128)(2,1)S(1)} %add_convert_fusion), channel_id=1, replica_groups=mesh['x'=4,'core'=2,'z'=16,'y'=4] {'x'}, dimensions={0} | all-to-all | bytes 2097152 | tf_op jit(solution)/shard_map/all_to_all | solution.py:103
  40.6 0.9 reduce_sum.24
  41.5 0.0 all-gather.2.cloned.1.call-update
  41.6 3.1 %collective-permute-start.1 = (bf16[4,64,1024]{2,1,0:T(8,128)(2,1)S(1)}, bf16[4,64,1024]{2,1,0:T(8,128)(2,1)S(1)}, u32[]{:S(2)}, u32[]{:S(2)}) collective-permute-start(bf16[4,64,1024]{2,1,0:T(8,128)(2,1)S(1)} %get-tuple-element.18), channel_id=1, source_target_pairs={{0,64},{64,0},{1,65},{65,1},{2,66},{66,2},{3,67},{67,3},{4,68},{68... | collective-permute-start | bytes 1572872 | tf_op jit(solution)/shard_map/ppermute | solution.py:101
  44.7 1.5 collective-permute-done.1
  46.2 1.0 add_convert_fusion.1
  47.2 3.5 %all-to-all-start.1 = ((bf16[4,64,1024]{2,1,0:T(8,128)(2,1)}), bf16[4,64,1024]{2,1,0:T(8,128)(2,1)S(1)}, u32[]{:S(2)}, u32[]{:S(2)}) async-start(bf16[4,64,1024]{2,1,0:T(8,128)(2,1)} %add_convert_fusion.1), calls=%async_computation.1 | async-start | bytes 1048576 | tf_op jit(solution)/shard_map/all_to_all | solution.py:103
  50.7 9.2 %all-to-all-done.1 = bf16[4,64,1024]{2,1,0:T(8,128)(2,1)S(1)} async-done(((bf16[4,64,1024]{2,1,0:T(8,128)(2,1)}), bf16[4,64,1024]{2,1,0:T(8,128)(2,1)S(1)}, u32[]{:S(2)}, u32[]{:S(2)}) %all-to-all-start.1) | async-done | bytes 524320 | tf_op jit(solution)/shard_map/all_to_all | solution.py:103
  59.9 0.1 reduce_sum.25
  59.9 50.9 %all-gather.2.cloned.1.call-done = bf16[2,1024,1024]{2,1,0:T(8,128)(2,1)} async-done(((bf16[2,64,1024]{2,1,0:T(8,128)(2,1)}), bf16[2,1024,1024]{2,1,0:T(8,128)(2,1)}) %all-gather.2.cloned.1.call-update) | async-done | bytes 4194320 | tf_op jit(solution)/shard_map/all_gather | solution.py:117
  110.8 1.6 %slice-done = bf16[1,1024,1024]{2,1,0:T(8,128)(2,1)S(1)} async-done(((bf16[2,1024,1024]{2,1,0:T(8,128)(2,1)}), bf16[1,1024,1024]{2,1,0:T(8,128)(2,1)S(1)}, s32[]{:S(2)}) %slice-start) | async-done | bytes 2097176 | tf_op jit(solution)/shard_map/slice | solution.py:120
  112.4 0.6 fusion.17
  113.1 3.1 %fusion.20 = bf16[1,64,1024]{2,1,0:T(8,128)(2,1)S(1)} fusion(bf16[2,1024,1024]{2,1,0:T(8,128)(2,1)} %all-gather.2.cloned.1.call-done, bf16[64,1024]{1,0:T(8,128)(2,1)S(1)} %reduce_sum.25), kind=kOutput, calls=%fused_computation.14 | convolution fusion | flops 268566528 | bytes 4456448 | tf_op jit(solution)/shard_map/dot_general | solution.py:122
  116.2 2.4 %fusion.21 = bf16[1,64,1024]{2,1,0:T(8,128)(2,1)S(1)} fusion(bf16[2,64,1024]{2,1,0:T(8,128)(2,1)S(1)} %copy-done.7, bf16[2,1024,1024]{2,1,0:T(8,128)(2,1)} %all-gather.2.cloned.1.call-done), kind=kOutput, calls=%fused_computation.15 | convolution fusion | flops 134283264 | bytes 2359296 | tf_op jit(solution)/shard_map/ik,jk->ij/dot_general | solution.py:123
  118.7 3.4 %collective-permute-start.3 = (bf16[3,64,1024]{2,1,0:T(8,128)(2,1)S(1)}, bf16[3,64,1024]{2,1,0:T(8,128)(2,1)S(1)}, u32[]{:S(2)}, u32[]{:S(2)}) collective-permute-start(bf16[3,64,1024]{2,1,0:T(8,128)(2,1)S(1)} %pad_maximum_fusion.refs_0_), channel_id=1, source_target_pairs={{0,128},{128,256},{256,384},{384,0},{1,129},{129,257},{257,385},{3... | collective-permute-start | bytes 1179656 | tf_op jit(solution)/shard_map/ppermute | solution.py:131
  122.1 4.5 %collective-permute-start.5 = (bf16[3,64,1024]{2,1,0:T(8,128)(2,1)S(1)}, bf16[3,64,1024]{2,1,0:T(8,128)(2,1)S(1)}, u32[]{:S(2)}, u32[]{:S(2)}) collective-permute-start(bf16[3,64,1024]{2,1,0:T(8,128)(2,1)S(1)} %pad_maximum_fusion.refs_0_), channel_id=1, source_target_pairs={{0,256},{128,384},{256,0},{384,128},{1,257},{129,385},{257,1},{385... | collective-permute-start | bytes 1179656 | tf_op jit(solution)/shard_map/ppermute | solution.py:131
  126.7 2.6 %collective-permute-start.7 = (bf16[3,64,1024]{2,1,0:T(8,128)(2,1)S(1)}, bf16[3,64,1024]{2,1,0:T(8,128)(2,1)S(1)}, u32[]{:S(2)}, u32[]{:S(2)}) collective-permute-start(bf16[3,64,1024]{2,1,0:T(8,128)(2,1)S(1)} %pad_maximum_fusion.refs_0_), channel_id=1, source_target_pairs={{0,384},{128,0},{256,128},{384,256},{1,385},{129,1},{257,129},{385... | collective-permute-start | bytes 1179656 | tf_op jit(solution)/shard_map/ppermute | solution.py:131
  129.2 12.3 %collective-permute-start.2 = (bf16[3,64,1024]{2,1,0:T(8,128)(2,1)S(1)}, bf16[3,64,1024]{2,1,0:T(8,128)(2,1)S(1)}, u32[]{:S(2)}, u32[]{:S(2)}) collective-permute-start(bf16[3,64,1024]{2,1,0:T(8,128)(2,1)S(1)} %pad_maximum_fusion.refs_0_), channel_id=1, source_target_pairs={{0,64},{64,0},{1,65},{65,1},{2,66},{66,2},{3,67},{67,3},{4,68},{68... | collective-permute-start | bytes 1179656 | tf_op jit(solution)/shard_map/ppermute | solution.py:132
  141.5 1.9 %collective-permute-start.4 = (bf16[3,64,1024]{2,1,0:T(8,128)(2,1)S(1)}, bf16[3,64,1024]{2,1,0:T(8,128)(2,1)S(1)}, u32[]{:S(2)}, u32[]{:S(2)}) collective-permute-start(bf16[3,64,1024]{2,1,0:T(8,128)(2,1)S(1)} %collective-permute-done.3.refs_2_), channel_id=1, source_target_pairs={{0,64},{64,0},{1,65},{65,1},{2,66},{66,2},{3,67},{67,3},{4,68},{68... | collective-permute-start | bytes 1179656 | tf_op jit(solution)/shard_map/ppermute | solution.py:132
  143.5 2.7 %collective-permute-start.6 = (bf16[3,64,1024]{2,1,0:T(8,128)(2,1)S(1)}, bf16[3,64,1024]{2,1,0:T(8,128)(2,1)S(1)}, u32[]{:S(2)}, u32[]{:S(2)}) collective-permute-start(bf16[3,64,1024]{2,1,0:T(8,128)(2,1)S(1)} %collective-permute-done.5.refs_4_), channel_id=1, source_target_pairs={{0,64},{64,0},{1,65},{65,1},{2,66},{66,2},{3,67},{67,3},{4,68},{68... | collective-permute-start | bytes 1179656 | tf_op jit(solution)/shard_map/ppermute | solution.py:132
  146.2 1.9 %collective-permute-start.8 = (bf16[3,64,1024]{2,1,0:T(8,128)(2,1)S(1)}, bf16[3,64,1024]{2,1,0:T(8,128)(2,1)S(1)}, u32[]{:S(2)}, u32[]{:S(2)}) collective-permute-start(bf16[3,64,1024]{2,1,0:T(8,128)(2,1)S(1)} %collective-permute-done.7.refs_6_), channel_id=1, source_target_pairs={{0,64},{64,0},{1,65},{65,1},{2,66},{66,2},{3,67},{67,3},{4,68},{68... | collective-permute-start | bytes 1179656 | tf_op jit(solution)/shard_map/ppermute | solution.py:132
  148.1 1.7 %collective-permute-done.8.refs_7_ = bf16[3,64,1024]{2,1,0:T(8,128)(2,1)S(1)} collective-permute-done((bf16[3,64,1024]{2,1,0:T(8,128)(2,1)S(1)}, bf16[3,64,1024]{2,1,0:T(8,128)(2,1)S(1)}, u32[]{:S(2)}, u32[]{:S(2)}) %collective-permute-start.8) | collective-permute-done | bytes 393248 | tf_op jit(solution)/shard_map/ppermute | solution.py:132
  149.8 2.2 %unpack.1 = (bf16[8,64,1024]{2,1,0:T(8,128)(2,1)}, f32[2,64,1024]{2,1,0:T(8,128)}, f32[2,64,1024]{2,1,0:T(8,128)}) custom-call(s32[4,8]{1,0:T(4,128)S(1)} %bitcast.54, f32[2,64,1024]{2,1,0:T(8,128)S(1)} %bitcast.49, f32[2,64,1024]{2,1,0:T(8,128)S(1)} %bitcast.50, bf16[3,64,1024]{2,1,0:T(8,128)(2,1)S(1)} %pad_maximum_fusion.refs_0_, ...), custom_call_target="tpu_custom_call" | custom-call | tf_op jit(solution)/shard_map/unpack/pallas_call | solution.py:90
  (20 shorter events, 0.1 us)
Async XLA Ops:
  7.2 103.7 %all-gather.2.cloned.1.call-start = ((), (), s32[]{:S(2)}) async-start(), calls=%async_computation.2 | async-start | bytes 4456448 | tf_op jit(solution)/shard_map/all_gather | solution.py:117
  7.2 1.2 copy-start
  8.4 0.9 copy-start.3
  9.4 0.9 copy-start.4
  10.3 0.7 copy-start.5
  11.9 11.1 %collective-permute-start = (bf16[4,2,64,1024]{3,2,1,0:T(8,128)(2,1)S(1)}, bf16[4,2,64,1024]{3,2,1,0:T(8,128)(2,1)S(1)}, u32[]{:S(2)}, u32[]{:S(2)}) collective-permute-start(bf16[4,2,64,1024]{3,2,1,0:T(8,128)(2,1)S(1)} %get-tuple-element.16), channel_id=1, source_target_pairs={{0,64},{64,0},{1,65},{65,1},{2,66},{66,2},{3,67},{67,3},{4,68},{68... | collective-permute-start | bytes 3145736 | tf_op jit(solution)/shard_map/ppermute | solution.py:101
  41.6 4.6 %collective-permute-start.1 = (bf16[4,64,1024]{2,1,0:T(8,128)(2,1)S(1)}, bf16[4,64,1024]{2,1,0:T(8,128)(2,1)S(1)}, u32[]{:S(2)}, u32[]{:S(2)}) collective-permute-start(bf16[4,64,1024]{2,1,0:T(8,128)(2,1)S(1)} %get-tuple-element.18), channel_id=1, source_target_pairs={{0,64},{64,0},{1,65},{65,1},{2,66},{66,2},{3,67},{67,3},{4,68},{68... | collective-permute-start | bytes 1572872 | tf_op jit(solution)/shard_map/ppermute | solution.py:101
  47.2 12.7 %all-to-all-start.1 = ((bf16[4,64,1024]{2,1,0:T(8,128)(2,1)}), bf16[4,64,1024]{2,1,0:T(8,128)(2,1)S(1)}, u32[]{:S(2)}, u32[]{:S(2)}) async-start(bf16[4,64,1024]{2,1,0:T(8,128)(2,1)} %add_convert_fusion.1), calls=%async_computation.1 | async-start | bytes 1048576 | tf_op jit(solution)/shard_map/all_to_all | solution.py:103
  110.8 1.6 %slice-start = ((bf16[2,1024,1024]{2,1,0:T(8,128)(2,1)}), bf16[1,1024,1024]{2,1,0:T(8,128)(2,1)S(1)}, s32[]{:S(2)}) async-start(bf16[2,1024,1024]{2,1,0:T(8,128)(2,1)} %all-gather.2.cloned.1.call-done), calls=%async_computation.3 | async-start | bytes 4194304 | tf_op jit(solution)/shard_map/slice | solution.py:120
  113.0 3.1 %copy-start.7 = (bf16[2,64,1024]{2,1,0:T(8,128)(2,1)S(1)}, bf16[2,64,1024]{2,1,0:T(8,128)(2,1)}, u32[]{:S(2)}) copy-start(bf16[2,64,1024]{2,1,0:T(8,128)(2,1)} %reduce_sum.24) | copy-start | bytes 786436
  116.2 33.6 %copy-start.1 = (f32[1,1,2,64,1024]{4,3,2,1,0:T(8,128)S(1)}, f32[1,1,2,64,1024]{4,3,2,1,0:T(8,128)}, u32[]{:S(2)}) copy-start(f32[1,1,2,64,1024]{4,3,2,1,0:T(8,128)} %param.8) | copy-start | bytes 1572868
  116.2 33.6 %copy-start.2 = (f32[1,1,2,64,1024]{4,3,2,1,0:T(8,128)S(1)}, f32[1,1,2,64,1024]{4,3,2,1,0:T(8,128)}, u32[]{:S(2)}) copy-start(f32[1,1,2,64,1024]{4,3,2,1,0:T(8,128)} %param.9) | copy-start | bytes 1572868
  116.2 33.6 %copy-start.6 = (s32[4,8,1]{1,2,0:T(1,128)S(1)}, s32[4,8,1]{1,2,0:T(1,128)}, u32[]{:S(2)}) copy-start(s32[4,8,1]{1,2,0:T(1,128)} %param.7) | copy-start | bytes 388
  118.7 22.8 %collective-permute-start.3 = (bf16[3,64,1024]{2,1,0:T(8,128)(2,1)S(1)}, bf16[3,64,1024]{2,1,0:T(8,128)(2,1)S(1)}, u32[]{:S(2)}, u32[]{:S(2)}) collective-permute-start(bf16[3,64,1024]{2,1,0:T(8,128)(2,1)S(1)} %pad_maximum_fusion.refs_0_), channel_id=1, source_target_pairs={{0,128},{128,256},{256,384},{384,0},{1,129},{129,257},{257,385},{3... | collective-permute-start | bytes 1179656 | tf_op jit(solution)/shard_map/ppermute | solution.py:131
  122.1 21.3 %collective-permute-start.5 = (bf16[3,64,1024]{2,1,0:T(8,128)(2,1)S(1)}, bf16[3,64,1024]{2,1,0:T(8,128)(2,1)S(1)}, u32[]{:S(2)}, u32[]{:S(2)}) collective-permute-start(bf16[3,64,1024]{2,1,0:T(8,128)(2,1)S(1)} %pad_maximum_fusion.refs_0_), channel_id=1, source_target_pairs={{0,256},{128,384},{256,0},{384,128},{1,257},{129,385},{257,1},{385... | collective-permute-start | bytes 1179656 | tf_op jit(solution)/shard_map/ppermute | solution.py:131
  126.7 19.5 %collective-permute-start.7 = (bf16[3,64,1024]{2,1,0:T(8,128)(2,1)S(1)}, bf16[3,64,1024]{2,1,0:T(8,128)(2,1)S(1)}, u32[]{:S(2)}, u32[]{:S(2)}) collective-permute-start(bf16[3,64,1024]{2,1,0:T(8,128)(2,1)S(1)} %pad_maximum_fusion.refs_0_), channel_id=1, source_target_pairs={{0,384},{128,0},{256,128},{384,256},{1,385},{129,1},{257,129},{385... | collective-permute-start | bytes 1179656 | tf_op jit(solution)/shard_map/ppermute | solution.py:131
  129.2 18.8 %collective-permute-start.2 = (bf16[3,64,1024]{2,1,0:T(8,128)(2,1)S(1)}, bf16[3,64,1024]{2,1,0:T(8,128)(2,1)S(1)}, u32[]{:S(2)}, u32[]{:S(2)}) collective-permute-start(bf16[3,64,1024]{2,1,0:T(8,128)(2,1)S(1)} %pad_maximum_fusion.refs_0_), channel_id=1, source_target_pairs={{0,64},{64,0},{1,65},{65,1},{2,66},{66,2},{3,67},{67,3},{4,68},{68... | collective-permute-start | bytes 1179656 | tf_op jit(solution)/shard_map/ppermute | solution.py:132
  141.5 6.6 %collective-permute-start.4 = (bf16[3,64,1024]{2,1,0:T(8,128)(2,1)S(1)}, bf16[3,64,1024]{2,1,0:T(8,128)(2,1)S(1)}, u32[]{:S(2)}, u32[]{:S(2)}) collective-permute-start(bf16[3,64,1024]{2,1,0:T(8,128)(2,1)S(1)} %collective-permute-done.3.refs_2_), channel_id=1, source_target_pairs={{0,64},{64,0},{1,65},{65,1},{2,66},{66,2},{3,67},{67,3},{4,68},{68... | collective-permute-start | bytes 1179656 | tf_op jit(solution)/shard_map/ppermute | solution.py:132
  143.5 4.6 %collective-permute-start.6 = (bf16[3,64,1024]{2,1,0:T(8,128)(2,1)S(1)}, bf16[3,64,1024]{2,1,0:T(8,128)(2,1)S(1)}, u32[]{:S(2)}, u32[]{:S(2)}) collective-permute-start(bf16[3,64,1024]{2,1,0:T(8,128)(2,1)S(1)} %collective-permute-done.5.refs_4_), channel_id=1, source_target_pairs={{0,64},{64,0},{1,65},{65,1},{2,66},{66,2},{3,67},{67,3},{4,68},{68... | collective-permute-start | bytes 1179656 | tf_op jit(solution)/shard_map/ppermute | solution.py:132
  146.2 3.6 %collective-permute-start.8 = (bf16[3,64,1024]{2,1,0:T(8,128)(2,1)S(1)}, bf16[3,64,1024]{2,1,0:T(8,128)(2,1)S(1)}, u32[]{:S(2)}, u32[]{:S(2)}) collective-permute-start(bf16[3,64,1024]{2,1,0:T(8,128)(2,1)S(1)} %collective-permute-done.7.refs_6_), channel_id=1, source_target_pairs={{0,64},{64,0},{1,65},{65,1},{2,66},{66,2},{3,67},{67,3},{4,68},{68... | collective-permute-start | bytes 1179656 | tf_op jit(solution)/shard_map/ppermute | solution.py:132
Sparse Core Ops, SparseCore 0:
  41.7 69.1 all-gather.1

commit v2 on v1

v2 whole, which is shorter than its diff:
```python
import jax
import jax.numpy as jnp
from jax import lax
from jax.experimental import pallas as pl
from jax.experimental.pallas import tpu as pltpu
from jax.sharding import Mesh, PartitionSpec as P

F32 = jnp.float32
BF16 = jnp.bfloat16
F16 = jnp.float16
CORE_SWAP = ((0, 1), (1, 0))
VMEM = pl.BlockSpec(memory_space=pltpu.VMEM)
SMEM = pl.BlockSpec(memory_space=pltpu.SMEM)
PARAMS = pltpu.CompilerParams(vmem_limit_bytes=24 << 20)


def owner_and_slot(table_ref, column, q, blocks):
    owner = table_ref[column, q]
    slot = jnp.int32(0)
    for other in range(blocks):
        same = jnp.logical_and(table_ref[column, other] == owner, other < q)
        slot = slot + same.astype(jnp.int32)
    return owner, slot


def pack_kernel(table_ref, grads_ref, right_ref, left_ref, own_ref, sib_ref, places_ref):
    column = lax.axis_index("y")
    core = lax.axis_index("core")
    me = lax.axis_index("x") * 2 + core
    blocks = grads_ref.shape[0]
    for i in range(places_ref.shape[0]):
        places_ref[i] = jnp.int32(0)
    for chip in range(own_ref.shape[0]):
        for parity, out_ref in ((core, own_ref), (1 - core, sib_ref)):
            q = 2 * chip + parity
            out_ref[chip, 0] = grads_ref[q]
            owner, slot = owner_and_slot(table_ref, column, q, blocks)

            @pl.when(owner == me)
            def _():
                out_ref[chip, 1] = right_ref[slot]
                out_ref[chip, 2] = left_ref[slot]
                places_ref[2 * slot] = q
                places_ref[2 * slot + 1] = jnp.int32(1)

            @pl.when(owner != me)
            def _():
                out_ref[chip, 1:] = jnp.zeros((2,) + right_ref.shape[1:], right_ref.dtype)


def pack(table, grads, right, left, chips):
    rows, width = grads.shape[1:]
    shape = jax.ShapeDtypeStruct((chips, 3, rows, width), grads.dtype)
    return pl.pallas_call(
        pack_kernel,
        out_shape=(shape, shape, jax.ShapeDtypeStruct((2 * right.shape[0],), jnp.int32)),
        in_specs=[SMEM, VMEM, VMEM, VMEM],
        out_specs=(VMEM, VMEM, SMEM),
        compiler_params=PARAMS,
        name="pack",
    )(table, grads, right, left)


def route(own, sibling):
    swapped = lax.ppermute(sibling, "core", CORE_SWAP)
    pair = (own.astype(F32) + swapped.astype(F32)).astype(BF16)
    arrived = lax.all_to_all(pair, "x", split_axis=0, concat_axis=0, tiled=True)
    return jnp.sum(arrived, axis=0, dtype=F32).astype(BF16)


def gather(strips, axis):
    count = len(strips)
    rows, width = strips[0].shape
    wide = jnp.stack([strip.astype(F32) for strip in strips])
    top = jnp.maximum(jnp.max(jnp.abs(wide), axis=(1, 2), keepdims=True), 1e-30)
    power = jnp.floor(jnp.log2(top)) - 13.0
    scaled = (wide * jnp.exp2(-power)).astype(F16).reshape(count * rows, width)
    powers = jnp.zeros((8, width), F16)
    for i in range(count):
        powers = jnp.where(lax.broadcasted_iota(jnp.int32, (8, width), 0) == i, power[i].astype(F16), powers)
    sent = jnp.concatenate([scaled, powers])
    got = lax.all_gather(sent, axis, axis=0, tiled=False)
    factor = jnp.exp2(got[:, count * rows : count * rows + count, :1].astype(F32))
    return [
        got[:, i * rows : (i + 1) * rows].astype(F32) * factor[:, i : i + 1] for i in range(count)
    ]


def local(replica_grads, owner_table, stats_left, stats_right, left_root, right_root):
    local_grads = replica_grads[0]
    matrices, rows_blocks, rows, width = local_grads.shape
    chips = lax.axis_size("x")
    blocks = matrices * rows_blocks
    table = owner_table[:, :, 0]
    own, sibling, places = pack(
        table, local_grads.reshape(blocks, rows, width), right_root[0, 0], left_root[0, 0], chips
    )
    block_strip, right_strip, left_strip = route(own, sibling)
    whole_block, whole_right = gather([block_strip, right_strip], "z")
    whole_block = whole_block.astype(BF16).reshape(-1, width)
    whole_right = whole_right.astype(BF16).reshape(-1, width)
    product = jnp.dot(left_strip, whole_block, preferred_element_type=F32).astype(BF16)
    result = jnp.dot(product, whole_right, preferred_element_type=F32).astype(BF16)
    left_term = jnp.einsum("ik,jk->ij", block_strip, whole_block, preferred_element_type=F32)
    own_cols = lax.dynamic_slice_in_dim(whole_block, lax.axis_index("z") * rows, rows, 1)
    right_term = jnp.einsum("ki,kj->ij", own_cols, whole_block, preferred_element_type=F32)
    updates, left_terms, right_terms = gather([result, left_term, right_term], ("x", "core"))
    update = updates.astype(BF16)
    new_left, new_right = [], []
    for slot in range(stats_left.shape[2]):
        place, owned = places[2 * slot], places[2 * slot + 1] > 0
        for terms, stats, new in ((left_terms, stats_left, new_left), (right_terms, stats_right, new_right)):
            term = lax.dynamic_index_in_dim(terms, place, 0, keepdims=False)
            new.append(stats[0, 0, slot] + jnp.where(owned, term, 0.0))
    new_left, new_right = jnp.stack(new_left), jnp.stack(new_right)
    return (
        update.reshape(matrices, rows_blocks, rows, width),
        new_left[None, None],
        new_right[None, None],
    )


def solution(mesh):
    replicas, shards, columns = mesh.devices.shape
    split = Mesh(
        mesh.devices.reshape(replicas // 2, 2, shards, columns), ("x", "core", "z", "y")
    )
    replica = ("x", "core")
    owned = P(replica, "y", None, "z", None)
    return jax.shard_map(
        local,
        mesh=split,
        in_specs=(P(replica, None, None, "z", "y"), P(), owned, owned, owned, owned),
        out_specs=(P(None, None, "z", "y"), owned, owned),
        check_vma=False,
    )
```

time: 159 us -> 145 us (0.912)
  blocking collectives: 17.3 us -> 84 us
  waiting for transfers between devices: 65.5 us -> 17.8 us
  starting transfers between devices: 44.7 us -> 12.3 us
  other arithmetic: 2.46 us -> 13.2 us
  between operations: 14.3 us -> 5.86 us
  matrix products: 6.16 us -> 3.82 us
    all_gather x0 -> x2, blocking collectives: none -> 84 us  [gather(): got = lax.all_gather(sent, axis, axis=0, tiled=False)]
    all_gather x1 -> x0, waiting for transfers between devices: 50.9 us -> none  [local(): whole = lax.all_gather(strips, 'z', axis=1, tiled=True)]
    ppermute x7 -> x0, starting transfers between devices: 29.3 us -> none  [the longest x4 18.8 us: local(): pieces += [piece, lax.ppermute(piece, 'core', CORE_SWAP)]]
    all_to_all x1 -> x0, blocking collectives: 17.3 us -> none  [route(): arrived = lax.all_to_all(pair, 'x', split_axis=0, concat_axis=0, tiled=True)]
    all_to_all x1, waiting for transfers between devices: 9.19 us -> 14.7 us  [route(): arrived = lax.all_to_all(pair, 'x', split_axis=0, concat_axis=0, tiled=True)]
    select_n x0 -> x4, other arithmetic: none -> 3.39 us  [gather(): jnp.where(lax.broadcasted_iota(jnp.int32, (8, width), 0) == i, power[i].a...]
    convert_element_type x0 -> x3, other arithmetic: none -> 3.22 us  [the longest x1 2.97 us: local(): whole_right = whole_right.astype(BF16).reshape(-1, width)]
    ppermute x2 -> x1, starting transfers between devices: 11.9 us -> 8.79 us  [route(): swapped = lax.ppermute(sibling, 'core', CORE_SWAP)]
  transfers between devices with their start and end apart: 11 -> 2, of which waited for: 5 -> 2; matrix products, arithmetic and copies ran while one was open for 1% -> 0% of each run, Pallas kernels for 0% -> 0%
where the time goes in v2:
time: 145 us
  blocking collectives  84 us (58%)
  waiting for transfers between devices  17.8 us (12%)
  other arithmetic  13.2 us (9%)
  starting transfers between devices  12.3 us (8%)
  local copies, waits for them, and re-layouts  6.27 us (4%)
  between operations  5.86 us (4%)
  matrix products  3.82 us (3%)
    all_gather x2, blocking collectives, gather(): got = lax.all_gather(sent, axis, axis=0, tiled=False)  84 us
    all_to_all x1, waiting for transfers between devices, route(): arrived = lax.all_to_all(pair, 'x', split_axis=0, concat_axis=0, tiled=True)  14.7 us
    ppermute x1, starting transfers between devices, route(): swapped = lax.ppermute(sibling, 'core', CORE_SWAP)  8.79 us
    unnamed x12, local copies, waits for them, and re-layouts  3.81 us
    all_to_all x1, starting transfers between devices, route(): arrived = lax.all_to_all(pair, 'x', split_axis=0, concat_axis=0, tiled=True)  3.56 us
    select_n x4, other arithmetic, gather(): jnp.where(lax.broadcasted_iota(jnp.int32, (8, width), 0) == i, power[i].a...  3.39 us
    ppermute x1, waiting for transfers between devices, route(): swapped = lax.ppermute(sibling, 'core', CORE_SWAP)  3.01 us
    convert_element_type x1, other arithmetic, local(): whole_right = whole_right.astype(BF16).reshape(-1, width)  2.97 us
  transfers between devices with their start and end apart: 2, of which 2 were waited for; matrix products, arithmetic and copies ran while one was open for 0% of the time, Pallas kernels for 0%

profile of v2, /device:TPU:1, one launch (start us, length us, event | category | flops | bytes accessed | tf_op | source)
XLA Modules:
  0.0 144.7 jit_solution(2918754557850150004)
XLA Ops:
  0.6 1.2 copy-done
  1.9 0.9 copy-done.1
  2.8 0.9 copy-done.2
  3.8 0.7 copy-done.3
  4.4 1.4 pack.1
  5.9 8.8 %collective-permute-start = (bf16[4,3,64,1024]{3,2,1,0:T(8,128)(2,1)S(1)}, bf16[4,3,64,1024]{3,2,1,0:T(8,128)(2,1)S(1)}, u32[]{:S(2)}, u32[]{:S(2)}) collective-permute-start(bf16[4,3,64,1024]{3,2,1,0:T(8,128)(2,1)S(1)} %get-tuple-element.7), channel_id=1, source_target_pairs={{0,64},{64,0},{1,65},{65,1},{2,66},{66,2},{3,67},{67,3},{4,68},{68... | collective-permute-start | bytes 4718600 | tf_op jit(solution)/shard_map/ppermute | solution.py:65
  14.7 3.0 %collective-permute-done = bf16[4,3,64,1024]{3,2,1,0:T(8,128)(2,1)S(1)} collective-permute-done((bf16[4,3,64,1024]{3,2,1,0:T(8,128)(2,1)S(1)}, bf16[4,3,64,1024]{3,2,1,0:T(8,128)(2,1)S(1)}, u32[]{:S(2)}, u32[]{:S(2)}) %collective-permute-start) | collective-permute-done | bytes 1572896 | tf_op jit(solution)/shard_map/ppermute | solution.py:65
  17.7 1.8 %add_convert_fusion = bf16[4,3,64,1024]{3,2,1,0:T(8,128)(2,1)} fusion(bf16[4,3,64,1024]{3,2,1,0:T(8,128)(2,1)S(1)} %collective-permute-done, bf16[4,3,64,1024]{3,2,1,0:T(8,128)(2,1)S(1)} %get-tuple-element.6), kind=kLoop, calls=%fused_computation.2 | loop fusion | flops 3145728 | bytes 4718592 | tf_op jit(solution)/shard_map/convert_element_type | solution.py:66
  19.5 3.6 %all-to-all-start = ((bf16[4,3,64,1024]{3,2,1,0:T(8,128)(2,1)}), bf16[4,3,64,1024]{3,2,1,0:T(8,128)(2,1)S(1)}, u32[]{:S(2)}, u32[]{:S(2)}) async-start(bf16[4,3,64,1024]{3,2,1,0:T(8,128)(2,1)} %add_convert_fusion), calls=%async_computation | async-start | bytes 3145728 | tf_op jit(solution)/shard_map/all_to_all | solution.py:67
  23.1 0.6 fusion.8
  28.8 14.7 %all-to-all-done = bf16[4,3,64,1024]{3,2,1,0:T(8,128)(2,1)S(1)} async-done(((bf16[4,3,64,1024]{3,2,1,0:T(8,128)(2,1)}), bf16[4,3,64,1024]{3,2,1,0:T(8,128)(2,1)S(1)}, u32[]{:S(2)}, u32[]{:S(2)}) %all-to-all-start) | async-done | bytes 1572896 | tf_op jit(solution)/shard_map/all_to_all | solution.py:67
  43.5 0.3 reduce_sum.12
  44.0 0.6 fusion.10
  44.6 0.7 compare_select_fusion.1
  45.6 0.7 broadcast_select_fusion
  46.4 58.9 %all-gather.4 = f16[2176,1024]{1,0:T(8,128)(2,1)S(1)} all-gather(f16[136,1024]{1,0:T(8,128)(2,1)S(1)} %pad_maximum_fusion.2), channel_id=2, replica_groups=mesh['x'=4,'core'=2,'z'=16,'y'=4] {'z'}, dimensions={0}, use_global_device_ids=true | all-gather | bytes 4734976 | tf_op jit(solution)/shard_map/all_gather | solution.py:82
  105.3 0.2 slice_reduce_fusion
  105.5 3.0 %multiply_convert_fusion = (bf16[16,64,1024]{2,1,0:T(8,128)(2,1)}, bf16[16,64,1024]{2,1,0:T(8,128)(2,1)S(1)}) fusion(f16[16,136,1024]{2,1,0:T(8,128)(2,1)S(1)} %bitcast.66, f32[16]{0:T(128)S(1)} %get-tuple-element.12, f32[16]{0:T(128)S(1)} %get-tuple-element.13), kind=kLoop, calls=%fused_computation | loop fusion | flops 6291456 | bytes 8388736 | tf_op jit(solution)/shard_map/convert_element_type | solution.py:101
  108.5 0.8 convolution_bitcast_fusion.1
  109.2 2.4 %fusion.1 = f32[1,64,1024]{2,1,0:T(8,128)S(1)} fusion(bf16[1024,1024]{1,0:T(8,128)(2,1)} %bitcast.69, bf16[1024,1024]{1,0:T(8,128)(2,1)S(1)} %bitcast.63, bf16[3,64,1024]{2,1,0:T(8,128)(2,1)S(1)} %reduce_sum.12), kind=kOutput, calls=%fused_computation.11 | convolution fusion | flops 268632064 | bytes 4587520 | tf_op jit(solution)/shard_map/dot_general | solution.py:103
  111.7 0.6 convolution_bitcast_fusion
  112.3 0.1 pad_maximum_fusion
  112.6 0.6 fusion.9
  113.2 0.7 compare_select_fusion
  113.9 0.1 fusion.2
  114.0 1.4 select_select_fusion
  115.5 25.1 %all-gather.5 = f16[1600,1024]{1,0:T(8,128)(2,1)S(1)} all-gather(f16[200,1024]{1,0:T(8,128)(2,1)S(1)} %pad_maximum_fusion.1), channel_id=3, replica_groups=mesh['x'=4,'core'=2,'z'=16,'y'=4] {'x','core'}, dimensions={0}, use_global_device_ids=true | all-gather | bytes 3686400 | tf_op jit(solution)/shard_map/all_gather | solution.py:82
  140.6 0.1 slice_reduce_fusion.2
  140.8 2.0 %convert_multiply_fusion = (f32[8,64,1024]{2,1,0:T(8,128)S(1)}, f32[8,64,1024]{2,1,0:T(8,128)S(1)}, bf16[8,64,1024]{2,1,0:T(8,128)(2,1)}) fusion(f16[8,200,1024]{2,1,0:T(8,128)(2,1)S(1)} %bitcast.68, f32[8]{0:T(128)S(1)} %get-tuple-element.9, f32[8]{0:T(128)S(1)} %get-tuple-element.10, f32[8]{0:T(128)S(1)} %get-tuple-element.11), kind=kLoop, calls=%fused_computation.3 | loop fusion | flops 3670016 | bytes 8388704 | tf_op jit(solution)/shard_map/mul | solution.py:85
  142.8 0.2 bitcast_add_fusion.1
  143.0 0.8 maximum_bitcast_fusion.1
  143.8 0.8 maximum_bitcast_fusion
  (23 shorter events, 0.8 us)
Async XLA Ops:
  0.6 1.2 copy-start
  1.9 0.9 copy-start.1
  2.8 0.9 copy-start.2
  3.8 0.7 copy-start.3
  5.9 11.8 %collective-permute-start = (bf16[4,3,64,1024]{3,2,1,0:T(8,128)(2,1)S(1)}, bf16[4,3,64,1024]{3,2,1,0:T(8,128)(2,1)S(1)}, u32[]{:S(2)}, u32[]{:S(2)}) collective-permute-start(bf16[4,3,64,1024]{3,2,1,0:T(8,128)(2,1)S(1)} %get-tuple-element.7), channel_id=1, source_target_pairs={{0,64},{64,0},{1,65},{65,1},{2,66},{66,2},{3,67},{67,3},{4,68},{68... | collective-permute-start | bytes 4718600 | tf_op jit(solution)/shard_map/ppermute | solution.py:65
  19.5 24.0 %all-to-all-start = ((bf16[4,3,64,1024]{3,2,1,0:T(8,128)(2,1)}), bf16[4,3,64,1024]{3,2,1,0:T(8,128)(2,1)S(1)}, u32[]{:S(2)}, u32[]{:S(2)}) async-start(bf16[4,3,64,1024]{3,2,1,0:T(8,128)(2,1)} %add_convert_fusion), calls=%async_computation | async-start | bytes 3145728 | tf_op jit(solution)/shard_map/all_to_all | solution.py:67
  140.8 2.0 %copy-start.4 = (f32[1,1,2,64,1024]{4,3,2,1,0:T(8,128)S(1)}, f32[1,1,2,64,1024]{4,3,2,1,0:T(8,128)}, u32[]{:S(2)}) copy-start(f32[1,1,2,64,1024]{4,3,2,1,0:T(8,128)} %param.9) | copy-start | bytes 1572868
  140.8 2.0 %copy-start.5 = (f32[1,1,2,64,1024]{4,3,2,1,0:T(8,128)S(1)}, f32[1,1,2,64,1024]{4,3,2,1,0:T(8,128)}, u32[]{:S(2)}) copy-start(f32[1,1,2,64,1024]{4,3,2,1,0:T(8,128)} %param.8) | copy-start | bytes 1572868

commit v3 on v2

v3 whole, which is shorter than its diff:
```python
import jax
import jax.numpy as jnp
from jax import lax
from jax.experimental import pallas as pl
from jax.experimental.pallas import tpu as pltpu
from jax.sharding import Mesh, PartitionSpec as P

F16 = jnp.float16
BF16 = jnp.bfloat16
F32 = jnp.float32
CORE_SWAP = ((0, 1), (1, 0))
VMEM = pl.BlockSpec(memory_space=pltpu.VMEM)
SMEM = pl.BlockSpec(memory_space=pltpu.SMEM)
PARAMS = pltpu.CompilerParams(vmem_limit_bytes=8 << 20)
POWER_ROWS = 8


def owner_and_slot(table_ref, column, q):
    owner = table_ref[column, q]
    slot = jnp.int32(0)
    for other in range(table_ref.shape[1]):
        same = jnp.logical_and(table_ref[column, other] == owner, other < q)
        slot = slot + same.astype(jnp.int32)
    return owner, slot


def pack_kernel(table_ref, grads_ref, right_root_ref, left_root_ref, swapped_ref, main_ref, places_ref):
    column = lax.axis_index("y")
    core = lax.axis_index("core")
    me = lax.axis_index("x") * 2 + core
    chips = main_ref.shape[0]
    slots = places_ref.shape[0] // 2
    for i in range(places_ref.shape[0]):
        places_ref[i] = jnp.int32(0)
    for q in range(2 * chips):
        owner, slot = owner_and_slot(table_ref, column, q)

        @pl.when(owner == me)
        def _():
            places_ref[2 * slot] = jnp.int32(q)
            places_ref[2 * slot + 1] = jnp.int32(1)

    for chip in range(chips):
        q = 2 * chip + core
        main_ref[chip, 0] = (grads_ref[q].astype(F32) + swapped_ref[chip].astype(F32)).astype(BF16)
        owner, slot = owner_and_slot(table_ref, column, q)

        @pl.when(owner == me)
        def _():
            main_ref[chip, 1] = right_root_ref[slot]
            main_ref[chip, 2] = left_root_ref[slot]

        @pl.when(owner == me + 1 - 2 * core)
        def _():
            main_ref[chip, 1] = swapped_ref[chips + slot]
            main_ref[chip, 2] = swapped_ref[chips + slots + slot]

        @pl.when(lax.shift_right_logical(owner, 1) != lax.axis_index("x"))
        def _():
            main_ref[chip, 1:] = jnp.zeros((2,) + main_ref.shape[2:], BF16)


def pack(table, grads, right, left, swapped, chips):
    rows, width = grads.shape[1:]
    slots = right.shape[0]
    return pl.pallas_call(
        pack_kernel,
        out_shape=(
            jax.ShapeDtypeStruct((chips, 3, rows, width), BF16),
            jax.ShapeDtypeStruct((2 * slots,), jnp.int32),
        ),
        in_specs=[SMEM] + [VMEM] * 4,
        out_specs=(VMEM, SMEM),
        compiler_params=PARAMS,
        name="pack",
    )(table, grads, right, left, swapped)


def put_scaled(out_ref, index, strip):
    rows, width = strip.shape
    top = jnp.max(jnp.max(jnp.abs(strip), axis=0, keepdims=True), axis=1, keepdims=True)
    power = jnp.floor(jnp.log2(jnp.maximum(top, 1e-30))) - 13.0
    out_ref[pl.ds(index * rows, rows), :] = strip * jnp.exp2(-power)
    return jnp.broadcast_to(power, (POWER_ROWS, width))


def put_powers(out_ref, powers):
    row = lax.broadcasted_iota(jnp.int32, (POWER_ROWS, out_ref.shape[1]), 0)
    block = powers[0]
    for i, power in enumerate(powers):
        block = jnp.where(row == i, power, block)
    out_ref[pl.ds(out_ref.shape[0] - POWER_ROWS, POWER_ROWS), :] = block


def scale_kernel(*refs):
    powers = [put_scaled(refs[-1], i, ref[...].astype(F32)) for i, ref in enumerate(refs[:-1])]
    put_powers(refs[-1], powers)


def scale_in_kernel(strips):
    rows, width = strips[0].shape
    return pl.pallas_call(
        scale_kernel,
        out_shape=jax.ShapeDtypeStruct((len(strips) * rows + POWER_ROWS, width), F32),
        in_specs=[VMEM] * len(strips),
        out_specs=VMEM,
        compiler_params=PARAMS,
        name="scale",
    )(*strips)


def scale(strips):
    rows, width = strips[0].shape
    wide = jnp.stack([strip.astype(F32) for strip in strips])
    top = jnp.maximum(jnp.max(jnp.abs(wide), axis=(1, 2), keepdims=True), 1e-30)
    power = jnp.floor(jnp.log2(top)) - 13.0
    scaled = (wide * jnp.exp2(-power)).astype(F16).reshape(len(strips) * rows, width)
    row = lax.broadcasted_iota(jnp.int32, (POWER_ROWS, width), 0)
    powers = jnp.zeros((POWER_ROWS, width), F16)
    for i in range(len(strips)):
        powers = jnp.where(row == i, power[i].astype(F16), powers)
    return jnp.concatenate([scaled, powers])


def gather(scaled, count, axis):
    got = lax.all_gather(scaled.astype(F16), axis, axis=0, tiled=False)
    body = got.shape[1] - POWER_ROWS
    rows = body // count
    factor = jnp.exp2(got[:, body : body + count, :1].astype(F32))
    return [
        got[:, i * rows : (i + 1) * rows].astype(F32) * factor[:, i : i + 1] for i in range(count)
    ]


def local(replica_grads, owner_table, stats_left, stats_right, left_root, right_root):
    local_grads = replica_grads[0]
    matrices, rows_blocks, rows, width = local_grads.shape
    chips = lax.axis_size("x")
    slots = stats_left.shape[2]
    blocks = matrices * rows_blocks
    grads = local_grads.reshape(blocks, rows, width)
    right, left = right_root[0, 0], left_root[0, 0]
    sibling = lax.dynamic_index_in_dim(
        grads.reshape(chips, 2, rows, width), 1 - lax.axis_index("core"), 1, keepdims=False
    )
    swapped = lax.ppermute(jnp.concatenate([sibling, right, left]), "core", CORE_SWAP)
    main, places = pack(owner_table[:, :, 0], grads, right, left, swapped, chips)
    arrived = lax.all_to_all(main, "x", split_axis=0, concat_axis=0, tiled=True)
    strips = jnp.sum(arrived, axis=0, dtype=F32).astype(BF16)
    scaled = scale([strips[0], strips[1]])
    whole_block, whole_right = gather(scaled, 2, "z")
    left_strip = strips[2]
    whole_block = whole_block.astype(BF16).reshape(-1, width)
    whole_right = whole_right.astype(BF16).reshape(-1, width)
    product = jnp.dot(left_strip, whole_block, preferred_element_type=F32).astype(BF16)
    result = jnp.dot(product, whole_right, preferred_element_type=F32).astype(BF16)
    left_term = jnp.einsum("ik,jk->ij", strips[0], whole_block, preferred_element_type=F32)
    own_cols = lax.dynamic_slice_in_dim(whole_block, lax.axis_index("z") * rows, rows, 1)
    right_term = jnp.einsum("ki,kj->ij", own_cols, whole_block, preferred_element_type=F32)
    updates, left_terms, right_terms = gather(
        scale_in_kernel([result, left_term, right_term]), 3, ("x", "core")
    )
    update = updates.astype(BF16)
    new_left, new_right = [], []
    for slot in range(slots):
        place, owned = places[2 * slot], places[2 * slot + 1] > 0
        for terms, stats, new in (
            (left_terms, stats_left, new_left),
            (right_terms, stats_right, new_right),
        ):
            term = lax.dynamic_index_in_dim(terms, place, 0, keepdims=False)
            new.append(stats[0, 0, slot] + jnp.where(owned, term, 0.0))
    return (
        update.reshape(matrices, rows_blocks, rows, width),
        jnp.stack(new_left)[None, None],
        jnp.stack(new_right)[None, None],
    )


def solution(mesh):
    replicas, shards, columns = mesh.devices.shape
    split = Mesh(
        mesh.devices.reshape(replicas // 2, 2, shards, columns), ("x", "core", "z", "y")
    )
    replica = ("x", "core")
    owned = P(replica, "y", None, "z", None)
    return jax.shard_map(
        local,
        mesh=split,
        in_specs=(P(replica, None, None, "z", "y"), P(), owned, owned, owned, owned),
        out_specs=(P(None, None, "z", "y"), owned, owned),
        check_vma=False,
    )
```

time: 145 us -> 139 us (0.959)
  local copies, waits for them, and re-layouts: 6.27 us -> 2.92 us
  other arithmetic: 13.2 us -> 10.1 us
    unnamed x12, local copies, waits for them, and re-layouts: 3.81 us -> 0.03 us
    select_n x4 -> x2, other arithmetic: 3.39 us -> 1.37 us  [scale(): powers = jnp.where(row == i, power[i].astype(F16), powers)]
    convert_element_type x4 -> x3, other arithmetic: 5.06 us -> 3.13 us  [the longest x1 2.96 us: local(): whole_block = whole_block.astype(BF16).reshape(-1, width)]
where the time goes in v3:
time: 139 us; the launch traced here: 138 us
  blocking collectives  84 us (60%)
  waiting for transfers between devices  17 us (12%)
  starting transfers between devices  12.4 us (9%)
  other arithmetic  10.1 us (7%)
  between operations  5.88 us (4%)
  matrix products  3.82 us (3%)
  local copies, waits for them, and re-layouts  2.92 us (2%)
  Pallas kernels  2.23 us (2%)
    all_gather x2, blocking collectives, gather(): got = lax.all_gather(scaled.astype(F16), axis, axis=0, tiled=False)  84 us
    all_to_all x1, waiting for transfers between devices, local(): arrived = lax.all_to_all(main, 'x', split_axis=0, concat_axis=0, tiled=True)  14.7 us
    ppermute x1, starting transfers between devices, local(): lax.ppermute(jnp.concatenate([sibling, right, left]), 'core', CORE_SWAP)  8.79 us
    all_to_all x1, starting transfers between devices, local(): arrived = lax.all_to_all(main, 'x', split_axis=0, concat_axis=0, tiled=True)  3.57 us
    convert_element_type x1, other arithmetic, local(): whole_block = whole_block.astype(BF16).reshape(-1, width)  2.96 us
  transfers between devices with their start and end apart: 2, of which 2 were waited for; matrix products, arithmetic and copies ran while one was open for 0% of the time, Pallas kernels for 0%

profile of v3, /device:TPU:1, one launch (start us, length us, event | category | flops | bytes accessed | tf_op | source)
XLA Modules:
  0.0 138.3 jit_solution(264376686001660728)
XLA Ops:
  0.6 0.0 copy-start.1
  0.7 1.2 dynamic-slice_bitcast_fusion
  1.9 1.2 pad_maximum_fusion
  3.0 8.8 %collective-permute-start = (bf16[8,64,1024]{2,1,0:T(8,128)(2,1)S(1)}, bf16[8,64,1024]{2,1,0:T(8,128)(2,1)S(1)}, u32[]{:S(2)}, u32[]{:S(2)}) collective-permute-start(bf16[8,64,1024]{2,1,0:T(8,128)(2,1)S(1)} %pad_maximum_fusion), channel_id=1, source_target_pairs={{0,64},{64,0},{1,65},{65,1},{2,66},{66,2},{3,67},{67,3},{4,68},{68... | collective-permute-start | bytes 3145736 | tf_op jit(solution)/shard_map/ppermute | solution.py:146
  11.8 2.3 %collective-permute-done.swapped_ref = bf16[8,64,1024]{2,1,0:T(8,128)(2,1)S(1)} collective-permute-done((bf16[8,64,1024]{2,1,0:T(8,128)(2,1)S(1)}, bf16[8,64,1024]{2,1,0:T(8,128)(2,1)S(1)}, u32[]{:S(2)}, u32[]{:S(2)}) %collective-permute-start) | collective-permute-done | bytes 1048608 | tf_op jit(solution)/shard_map/ppermute | solution.py:146
  14.1 2.0 %pack.1 = (bf16[4,3,64,1024]{3,2,1,0:T(8,128)(2,1)}, s32[4]{0:T(128)S(1)}) custom-call(s32[4,8]{1,0:T(4,128)S(1)} %bitcast.53, bf16[8,64,1024]{2,1,0:T(8,128)(2,1)S(1)} %bitcast.48, bf16[2,64,1024]{2,1,0:T(8,128)(2,1)S(1)} %bitcast.50, bf16[2,64,1024]{2,1,0:T(8,128)(2,1)S(1)} %bitcast.52, bf16[8,64,1024]{2,1,0:T(8,128)(2,1)S(1)} %collective-permute-done.swapped_ref), custom_call_target="tpu_custom_call" | custom-call | tf_op jit(solution)/shard_map/pack/pallas_call | solution.py:66
  16.1 3.6 %all-to-all-start = ((bf16[4,3,64,1024]{3,2,1,0:T(8,128)(2,1)}), bf16[4,3,64,1024]{3,2,1,0:T(8,128)(2,1)S(1)}, u32[]{:S(2)}, u32[]{:S(2)}) async-start(bf16[4,3,64,1024]{3,2,1,0:T(8,128)(2,1)} %get-tuple-element.5), calls=%async_computation | async-start | bytes 3145728 | tf_op jit(solution)/shard_map/all_to_all | solution.py:148
  19.7 0.6 fusion.6
  25.4 14.7 %all-to-all-done = bf16[4,3,64,1024]{3,2,1,0:T(8,128)(2,1)S(1)} async-done(((bf16[4,3,64,1024]{3,2,1,0:T(8,128)(2,1)}), bf16[4,3,64,1024]{3,2,1,0:T(8,128)(2,1)S(1)}, u32[]{:S(2)}, u32[]{:S(2)}) %all-to-all-start) | async-done | bytes 1572896 | tf_op jit(solution)/shard_map/all_to_all | solution.py:148
  40.1 0.3 reduce_sum.12
  40.5 0.1 abs_reduce_fusion
  40.7 0.6 fusion.7
  41.2 0.7 compare_select_fusion
  41.9 0.1 mul.66
  42.0 0.1 mul.67
  42.1 0.1 fusion
  42.2 0.7 broadcast_select_fusion
  42.9 0.1 pad_maximum_fusion.1
  43.0 58.9 %all-gather.4 = f16[2176,1024]{1,0:T(8,128)(2,1)S(1)} all-gather(f16[136,1024]{1,0:T(8,128)(2,1)S(1)} %pad_maximum_fusion.1), channel_id=2, replica_groups=mesh['x'=4,'core'=2,'z'=16,'y'=4] {'z'}, dimensions={0}, use_global_device_ids=true | all-gather | bytes 4734976 | tf_op jit(solution)/shard_map/all_gather | solution.py:126
  101.8 0.2 slice_reduce_fusion.1
  102.1 3.0 %multiply_convert_fusion.1 = (bf16[16,64,1024]{2,1,0:T(8,128)(2,1)S(1)}, bf16[16,64,1024]{2,1,0:T(8,128)(2,1)}) fusion(f16[16,136,1024]{2,1,0:T(8,128)(2,1)S(1)} %bitcast.58, f32[16]{0:T(128)S(1)} %get-tuple-element.10, f32[16]{0:T(128)S(1)} %get-tuple-element.11), kind=kLoop, calls=%fused_computation.1 | loop fusion | flops 6291456 | bytes 8388736 | tf_op jit(solution)/shard_map/convert_element_type | solution.py:153
  105.0 0.8 fusion.3.refs_1_
  105.8 0.6 fusion.1.refs_2_
  106.4 2.4 %convolution_convert_fusion.refs_0_ = bf16[64,1024]{1,0:T(8,128)(2,1)S(1)} fusion(bf16[1024,1024]{1,0:T(8,128)(2,1)} %bitcast.61, bf16[1024,1024]{1,0:T(8,128)(2,1)S(1)} %bitcast.56, bf16[3,64,1024]{2,1,0:T(8,128)(2,1)S(1)} %reduce_sum.12), kind=kOutput, calls=%fused_computation.5 | convolution fusion | flops 268566528 | bytes 4456448 | tf_op jit(solution)/shard_map/dot_general | solution.py:156
  108.9 0.2 scale.1
  109.0 0.1 convert_element_type.61
  109.1 25.1 %all-gather.5 = f16[1600,1024]{1,0:T(8,128)(2,1)S(1)} all-gather(f16[200,1024]{1,0:T(8,128)(2,1)S(1)} %convert_element_type.61), channel_id=3, replica_groups=mesh['x'=4,'core'=2,'z'=16,'y'=4] {'x','core'}, dimensions={0}, use_global_device_ids=true | all-gather | bytes 3686400 | tf_op jit(solution)/shard_map/all_gather | solution.py:126
  134.3 0.1 slice_reduce_fusion.2
  134.4 2.0 %convert_multiply_fusion = (f32[8,64,1024]{2,1,0:T(8,128)S(1)}, f32[8,64,1024]{2,1,0:T(8,128)S(1)}, bf16[8,64,1024]{2,1,0:T(8,128)(2,1)}) fusion(f16[8,200,1024]{2,1,0:T(8,128)(2,1)S(1)} %bitcast.60, f32[8]{0:T(128)S(1)} %get-tuple-element.7, f32[8]{0:T(128)S(1)} %get-tuple-element.8, f32[8]{0:T(128)S(1)} %get-tuple-element.9), kind=kLoop, calls=%fused_computation.2 | loop fusion | flops 3670016 | bytes 8388704 | tf_op jit(solution)/shard_map/mul | solution.py:131
  136.4 0.2 bitcast_add_fusion.1
  136.6 0.8 maximum_bitcast_fusion.1
  137.5 0.8 maximum_bitcast_fusion
  (16 shorter events, 0.1 us)
Async XLA Ops:
  0.6 13.5 %copy-start = (bf16[1,2,4,64,1024]{4,3,2,1,0:T(8,128)(2,1)S(1)}, bf16[1,2,4,64,1024]{4,3,2,1,0:T(8,128)(2,1)}, u32[]{:S(2)}) copy-start(bf16[1,2,4,64,1024]{4,3,2,1,0:T(8,128)(2,1)} %param.6) | copy-start | bytes 3145732
  0.6 13.5 %copy-start.1 = (bf16[1,1,2,64,1024]{4,3,2,1,0:T(8,128)(2,1)S(1)}, bf16[1,1,2,64,1024]{4,3,2,1,0:T(8,128)(2,1)}, u32[]{:S(2)}) copy-start(bf16[1,1,2,64,1024]{4,3,2,1,0:T(8,128)(2,1)} %param.11) | copy-start | bytes 786436
  0.7 13.4 %copy-start.2 = (bf16[1,1,2,64,1024]{4,3,2,1,0:T(8,128)(2,1)S(1)}, bf16[1,1,2,64,1024]{4,3,2,1,0:T(8,128)(2,1)}, u32[]{:S(2)}) copy-start(bf16[1,1,2,64,1024]{4,3,2,1,0:T(8,128)(2,1)} %param.10) | copy-start | bytes 786436
  0.7 13.4 %copy-start.3 = (s32[4,8,1]{1,2,0:T(1,128)S(1)}, s32[4,8,1]{1,2,0:T(1,128)}, u32[]{:S(2)}) copy-start(s32[4,8,1]{1,2,0:T(1,128)} %param.7) | copy-start | bytes 388
  3.0 11.1 %collective-permute-start = (bf16[8,64,1024]{2,1,0:T(8,128)(2,1)S(1)}, bf16[8,64,1024]{2,1,0:T(8,128)(2,1)S(1)}, u32[]{:S(2)}, u32[]{:S(2)}) collective-permute-start(bf16[8,64,1024]{2,1,0:T(8,128)(2,1)S(1)} %pad_maximum_fusion), channel_id=1, source_target_pairs={{0,64},{64,0},{1,65},{65,1},{2,66},{66,2},{3,67},{67,3},{4,68},{68... | collective-permute-start | bytes 3145736 | tf_op jit(solution)/shard_map/ppermute | solution.py:146
  16.1 24.0 %all-to-all-start = ((bf16[4,3,64,1024]{3,2,1,0:T(8,128)(2,1)}), bf16[4,3,64,1024]{3,2,1,0:T(8,128)(2,1)S(1)}, u32[]{:S(2)}, u32[]{:S(2)}) async-start(bf16[4,3,64,1024]{3,2,1,0:T(8,128)(2,1)} %get-tuple-element.5), calls=%async_computation | async-start | bytes 3145728 | tf_op jit(solution)/shard_map/all_to_all | solution.py:148
  134.4 2.0 %copy-start.4 = (f32[1,1,2,64,1024]{4,3,2,1,0:T(8,128)S(1)}, f32[1,1,2,64,1024]{4,3,2,1,0:T(8,128)}, u32[]{:S(2)}) copy-start(f32[1,1,2,64,1024]{4,3,2,1,0:T(8,128)} %param.9) | copy-start | bytes 1572868
  134.4 2.0 %copy-start.5 = (f32[1,1,2,64,1024]{4,3,2,1,0:T(8,128)S(1)}, f32[1,1,2,64,1024]{4,3,2,1,0:T(8,128)}, u32[]{:S(2)}) copy-start(f32[1,1,2,64,1024]{4,3,2,1,0:T(8,128)} %param.8) | copy-start | bytes 1572868

commit v4 on v3

--- a/solution.py
+++ b/solution.py
@@ -11,7 +11,7 @@
 CORE_SWAP = ((0, 1), (1, 0))
 VMEM = pl.BlockSpec(memory_space=pltpu.VMEM)
 SMEM = pl.BlockSpec(memory_space=pltpu.SMEM)
-PARAMS = pltpu.CompilerParams(vmem_limit_bytes=8 << 20)
+PARAMS = pltpu.CompilerParams(vmem_limit_bytes=16 << 20)
 POWER_ROWS = 8
 
 
@@ -24,22 +24,12 @@
     return owner, slot
 
 
-def pack_kernel(table_ref, grads_ref, right_root_ref, left_root_ref, swapped_ref, main_ref, places_ref):
+def pack_kernel(table_ref, grads_ref, right_root_ref, left_root_ref, swapped_ref, main_ref):
     column = lax.axis_index("y")
     core = lax.axis_index("core")
     me = lax.axis_index("x") * 2 + core
     chips = main_ref.shape[0]
-    slots = places_ref.shape[0] // 2
-    for i in range(places_ref.shape[0]):
-        places_ref[i] = jnp.int32(0)
-    for q in range(2 * chips):
-        owner, slot = owner_and_slot(table_ref, column, q)
-
-        @pl.when(owner == me)
-        def _():
-            places_ref[2 * slot] = jnp.int32(q)
-            places_ref[2 * slot + 1] = jnp.int32(1)
-
+    slots = right_root_ref.shape[0]
     for chip in range(chips):
         q = 2 * chip + core
         main_ref[chip, 0] = (grads_ref[q].astype(F32) + swapped_ref[chip].astype(F32)).astype(BF16)
@@ -62,18 +52,39 @@
 
 def pack(table, grads, right, left, swapped, chips):
     rows, width = grads.shape[1:]
-    slots = right.shape[0]
     return pl.pallas_call(
         pack_kernel,
-        out_shape=(
-            jax.ShapeDtypeStruct((chips, 3, rows, width), BF16),
-            jax.ShapeDtypeStruct((2 * slots,), jnp.int32),
-        ),
+        out_shape=jax.ShapeDtypeStruct((chips, 3, rows, width), BF16),
         in_specs=[SMEM] + [VMEM] * 4,
-        out_specs=(VMEM, SMEM),
+        out_specs=VMEM,
         compiler_params=PARAMS,
         name="pack",
     )(table, grads, right, left, swapped)
+
+
+def statistics_kernel(table_ref, *refs):
+    column = lax.axis_index("y")
+    me = lax.axis_index("x") * 2 + lax.axis_index("core")
+    for terms_ref, stats_ref, new_ref in zip(refs[:2], refs[2:4], refs[4:]):
+        new_ref[...] = stats_ref[...]
+        for q in range(terms_ref.shape[0]):
+            owner, slot = owner_and_slot(table_ref, column, q)
+
+            @pl.when(owner == me)
+            def _():
+                new_ref[slot] = stats_ref[slot] + terms_ref[q]
+
+
+def statistics(table, terms, stats):
+    shape = jax.ShapeDtypeStruct(stats[0].shape, F32)
+    return pl.pallas_call(
+        statistics_kernel,
+        out_shape=(shape, shape),
+        in_specs=[SMEM] + [VMEM] * 4,
+        out_specs=(VMEM, VMEM),
+        compiler_params=PARAMS,
+        name="statistics",
+    )(table, *terms, *stats)
 
 
 def put_scaled(out_ref, index, strip):
@@ -114,11 +125,9 @@
     wide = jnp.stack([strip.astype(F32) for strip in strips])
     top = jnp.maximum(jnp.max(jnp.abs(wide), axis=(1, 2), keepdims=True), 1e-30)
     power = jnp.floor(jnp.log2(top)) - 13.0
-    scaled = (wide * jnp.exp2(-power)).astype(F16).reshape(len(strips) * rows, width)
-    row = lax.broadcasted_iota(jnp.int32, (POWER_ROWS, width), 0)
-    powers = jnp.zeros((POWER_ROWS, width), F16)
-    for i in range(len(strips)):
-        powers = jnp.where(row == i, power[i].astype(F16), powers)
+    scaled = (wide * jnp.exp2(-power)).reshape(len(strips) * rows, width)
+    powers = jnp.broadcast_to(power[:, 0], (len(strips), width))
+    powers = jnp.pad(powers, ((0, POWER_ROWS - len(strips)), (0, 0)))
     return jnp.concatenate([scaled, powers])
 
 
@@ -136,15 +145,14 @@
     local_grads = replica_grads[0]
     matrices, rows_blocks, rows, width = local_grads.shape
     chips = lax.axis_size("x")
-    slots = stats_left.shape[2]
     blocks = matrices * rows_blocks
     grads = local_grads.reshape(blocks, rows, width)
     right, left = right_root[0, 0], left_root[0, 0]
-    sibling = lax.dynamic_index_in_dim(
-        grads.reshape(chips, 2, rows, width), 1 - lax.axis_index("core"), 1, keepdims=False
-    )
+    even, odd = grads.reshape(chips, 2, rows, width).transpose(1, 0, 2, 3)
+    sibling = jnp.where(lax.axis_index("core") == 0, odd, even)
     swapped = lax.ppermute(jnp.concatenate([sibling, right, left]), "core", CORE_SWAP)
-    main, places = pack(owner_table[:, :, 0], grads, right, left, swapped, chips)
+    table = owner_table[:, :, 0]
+    main = pack(table, grads, right, left, swapped, chips)
     arrived = lax.all_to_all(main, "x", split_axis=0, concat_axis=0, tiled=True)
     strips = jnp.sum(arrived, axis=0, dtype=F32).astype(BF16)
     scaled = scale([strips[0], strips[1]])
@@ -161,19 +169,13 @@
         scale_in_kernel([result, left_term, right_term]), 3, ("x", "core")
     )
     update = updates.astype(BF16)
-    new_left, new_right = [], []
-    for slot in range(slots):
-        place, owned = places[2 * slot], places[2 * slot + 1] > 0
-        for terms, stats, new in (
-            (left_terms, stats_left, new_left),
-            (right_terms, stats_right, new_right),
-        ):
-            term = lax.dynamic_index_in_dim(terms, place, 0, keepdims=False)
-            new.append(stats[0, 0, slot] + jnp.where(owned, term, 0.0))
+    new_left, new_right = statistics(
+        table, (left_terms, right_terms), (stats_left[0, 0], stats_right[0, 0])
+    )
     return (
         update.reshape(matrices, rows_blocks, rows, width),
-        jnp.stack(new_left)[None, None],
-        jnp.stack(new_right)[None, None],
+        new_left[None, None],
+        new_right[None, None],
     )
 
 

time: 139 us -> 136 us (0.978)
  waiting for transfers between devices: 17 us -> 22.7 us
  between operations: 5.88 us -> 0.82 us
  other arithmetic: 10.1 us -> 5.89 us
  Pallas kernels: 2.23 us -> 3.96 us
    all_to_all x1, waiting for transfers between devices: 14.7 us -> 20.4 us  [local(): arrived = lax.all_to_all(main, 'x', split_axis=0, concat_axis=0, tiled=True)]
    pallas_call x1 -> x2, Pallas kernels: 2.03 us -> 3.77 us  [the longest x1 1.96 us: pack(): pl.pallas_call(pack_kernel, out_shape=jax.ShapeDtypeStruct((chips, 3, row...]
    broadcast_in_dim x2 -> x0, other arithmetic: 1.66 us -> none  [the longest x1 0.83 us: local(): jnp.stack(new_right)[None, None]]
where the time goes in v4:
time: 136 us
  blocking collectives  84 us (62%)
  waiting for transfers between devices  22.7 us (17%)
  starting transfers between devices  12.5 us (9%)
  other arithmetic  5.89 us (4%)
  Pallas kernels  3.96 us (3%)
  matrix products  3.83 us (3%)
  local copies, waits for them, and re-layouts  1.93 us (1%)
    all_gather x2, blocking collectives, gather(): got = lax.all_gather(scaled.astype(F16), axis, axis=0, tiled=False)  84 us
    all_to_all x1, waiting for transfers between devices, local(): arrived = lax.all_to_all(main, 'x', split_axis=0, concat_axis=0, tiled=True)  20.4 us
    ppermute x1, starting transfers between devices, local(): lax.ppermute(jnp.concatenate([sibling, right, left]), 'core', CORE_SWAP)  8.92 us
    all_to_all x1, starting transfers between devices, local(): arrived = lax.all_to_all(main, 'x', split_axis=0, concat_axis=0, tiled=True)  3.56 us
    convert_element_type x1, other arithmetic, local(): whole_block = whole_block.astype(BF16).reshape(-1, width)  2.9 us
  transfers between devices with their start and end apart: 2, of which 2 were waited for; matrix products, arithmetic and copies ran while one was open for 0% of the time, Pallas kernels for 0%

profile of v4, /device:TPU:1, one launch (start us, length us, event | category | flops | bytes accessed | tf_op | source)
XLA Modules:
  0.0 135.6 jit_solution(129298508071530981)
XLA Ops:
  0.6 0.0 copy-start.1
  0.6 0.0 copy-start.2
  0.7 1.4 %copy.13 = bf16[4,2,64,1024]{3,2,0,1:T(8,128)(2,1)S(1)} copy(bf16[4,2,64,1024]{3,2,1,0:T(8,128)(2,1)} %bitcast.34) | data formatting | bytes 2097152 | tf_op jit(solution)/shard_map/reshape;reshape;squeeze | solution.py:151
  2.0 0.0 copy-start
  2.1 0.0 copy-start.5
  2.1 0.1 fusion
  2.1 0.0 copy-done.1
  2.2 0.1 pad_maximum_fusion
  2.3 8.9 %collective-permute-start = (bf16[8,64,1024]{2,1,0:T(8,128)(2,1)S(1)}, bf16[8,64,1024]{2,1,0:T(8,128)(2,1)S(1)}, u32[]{:S(2)}, u32[]{:S(2)}) collective-permute-start(bf16[8,64,1024]{2,1,0:T(8,128)(2,1)S(1)} %pad_maximum_fusion), channel_id=1, source_target_pairs={{0,64},{64,0},{1,65},{65,1},{2,66},{66,2},{3,67},{67,3},{4,68},{68... | collective-permute-start | bytes 3145736 | tf_op jit(solution)/shard_map/ppermute | solution.py:153
  11.2 2.3 %collective-permute-done.swapped_ref = bf16[8,64,1024]{2,1,0:T(8,128)(2,1)S(1)} collective-permute-done((bf16[8,64,1024]{2,1,0:T(8,128)(2,1)S(1)}, bf16[8,64,1024]{2,1,0:T(8,128)(2,1)S(1)}, u32[]{:S(2)}, u32[]{:S(2)}) %collective-permute-start) | collective-permute-done | bytes 1048608 | tf_op jit(solution)/shard_map/ppermute | solution.py:153
  13.5 2.0 %pack.1 = bf16[4,3,64,1024]{3,2,1,0:T(8,128)(2,1)} custom-call(s32[4,8]{1,0:T(4,128)S(1)} %bitcast.42, bf16[8,64,1024]{2,1,0:T(8,128)(2,1)S(1)} %bitcast.35, bf16[2,64,1024]{2,1,0:T(8,128)(2,1)S(1)} %bitcast.37, bf16[2,64,1024]{2,1,0:T(8,128)(2,1)S(1)} %bitcast.39, bf16[8,64,1024]{2,1,0:T(8,128)(2,1)S(1)} %collective-permute-done.swapped_ref), custom_call_target="tpu_custom_call" | custom-call | tf_op jit(solution)/shard_map/pack/pallas_call | solution.py:55
  15.4 3.6 %all-to-all-start = ((bf16[4,3,64,1024]{3,2,1,0:T(8,128)(2,1)}), bf16[4,3,64,1024]{3,2,1,0:T(8,128)(2,1)S(1)}, u32[]{:S(2)}, u32[]{:S(2)}) async-start(bf16[4,3,64,1024]{3,2,1,0:T(8,128)(2,1)} %pack.1), calls=%async_computation | async-start | bytes 3145728 | tf_op jit(solution)/shard_map/all_to_all | solution.py:156
  19.0 20.4 %all-to-all-done = bf16[4,3,64,1024]{3,2,1,0:T(8,128)(2,1)S(1)} async-done(((bf16[4,3,64,1024]{3,2,1,0:T(8,128)(2,1)}), bf16[4,3,64,1024]{3,2,1,0:T(8,128)(2,1)S(1)}, u32[]{:S(2)}, u32[]{:S(2)}) %all-to-all-start) | async-done | bytes 1572896 | tf_op jit(solution)/shard_map/all_to_all | solution.py:156
  39.4 0.3 reduce_sum.12
  39.8 0.1 abs_reduce_fusion
  40.0 0.1 mul.72
  40.0 0.1 mul.73
  40.1 0.1 fusion.1
  40.3 0.1 pad_maximum_fusion.1
  40.4 58.9 %all-gather.3 = f16[16,136,1024]{2,1,0:T(8,128)(2,1)S(1)} all-gather(f16[1,136,1024]{2,1,0:T(8,128)(2,1)S(1)} %pad_maximum_fusion.1), channel_id=1, replica_groups=mesh['x'=4,'core'=2,'z'=16,'y'=4] {'z'}, dimensions={0}, use_global_device_ids=true | all-gather | bytes 4734976 | tf_op jit(solution)/shard_map/all_gather | solution.py:135
  99.3 0.2 slice_reduce_fusion.1
  99.5 2.9 %multiply_convert_fusion.1 = (bf16[16,64,1024]{2,1,0:T(8,128)(2,1)S(1)}, bf16[16,64,1024]{2,1,0:T(8,128)(2,1)}) fusion(f16[16,136,1024]{2,1,0:T(8,128)(2,1)S(1)} %all-gather.3, f32[16]{0:T(128)S(1)} %get-tuple-element.10, f32[16]{0:T(128)S(1)} %get-tuple-element.11), kind=kLoop, calls=%fused_computation.1 | loop fusion | flops 6291456 | bytes 8388736 | tf_op jit(solution)/shard_map/convert_element_type | solution.py:161
  102.4 0.8 fusion.4.refs_1_
  103.2 2.4 %convolution_convert_fusion.refs_0_ = bf16[64,1024]{1,0:T(8,128)(2,1)S(1)} fusion(bf16[1024,1024]{1,0:T(8,128)(2,1)} %bitcast.49, bf16[1024,1024]{1,0:T(8,128)(2,1)S(1)} %bitcast.45, bf16[3,64,1024]{2,1,0:T(8,128)(2,1)S(1)} %reduce_sum.12), kind=kOutput, calls=%fused_computation.5 | convolution fusion | flops 268566528 | bytes 4456448 | tf_op jit(solution)/shard_map/dot_general | solution.py:164
  105.6 0.6 fusion.2.refs_2_
  106.2 0.2 scale.1
  106.4 0.1 convert_element_type.62
  106.5 25.1 %all-gather.4 = f16[1600,1024]{1,0:T(8,128)(2,1)S(1)} all-gather(f16[200,1024]{1,0:T(8,128)(2,1)S(1)} %convert_element_type.62), channel_id=2, replica_groups=mesh['x'=4,'core'=2,'z'=16,'y'=4] {'x','core'}, dimensions={0}, use_global_device_ids=true | all-gather | bytes 3686400 | tf_op jit(solution)/shard_map/all_gather | solution.py:135
  131.6 0.1 slice_reduce_fusion.2
  131.8 0.0 copy-start.4
  131.8 2.0 %convert_multiply_fusion = (f32[8,64,1024]{2,1,0:T(8,128)S(1)}, f32[8,64,1024]{2,1,0:T(8,128)S(1)}, bf16[8,64,1024]{2,1,0:T(8,128)(2,1)}) fusion(f16[8,200,1024]{2,1,0:T(8,128)(2,1)S(1)} %bitcast.48, f32[8]{0:T(128)S(1)} %get-tuple-element.7, f32[8]{0:T(128)S(1)} %get-tuple-element.8, f32[8]{0:T(128)S(1)} %get-tuple-element.9), kind=kLoop, calls=%fused_computation.2 | loop fusion | flops 3670016 | bytes 8388704 | tf_op jit(solution)/shard_map/mul | solution.py:140
  133.8 1.8 %statistics.1 = (f32[2,64,1024]{2,1,0:T(8,128)}, f32[2,64,1024]{2,1,0:T(8,128)}) custom-call(s32[4,8]{1,0:T(4,128)S(1)} %bitcast.43, f32[8,64,1024]{2,1,0:T(8,128)S(1)} %get-tuple-element.17.refs_0_, f32[8,64,1024]{2,1,0:T(8,128)S(1)} %get-tuple-element.16.refs_1_, f32[2,64,1024]{2,1,0:T(8,128)S(1)} %bitcast.40, f32[2,64,1024]{2,1,0:T(8,128)S(1)} %bitcast.41), custom_call_target="tpu_custom_call" | custom-call | tf_op jit(solution)/shard_map/statistics/pallas_call | solution.py:80
  (12 shorter events, 0.1 us)
Async XLA Ops:
  0.6 1.5 %copy-start.1 = (bf16[1,1,2,64,1024]{4,3,2,1,0:T(8,128)(2,1)S(1)}, bf16[1,1,2,64,1024]{4,3,2,1,0:T(8,128)(2,1)}, u32[]{:S(2)}) copy-start(bf16[1,1,2,64,1024]{4,3,2,1,0:T(8,128)(2,1)} %param.11) | copy-start | bytes 786436
  0.6 1.5 %copy-start.2 = (bf16[1,1,2,64,1024]{4,3,2,1,0:T(8,128)(2,1)S(1)}, bf16[1,1,2,64,1024]{4,3,2,1,0:T(8,128)(2,1)}, u32[]{:S(2)}) copy-start(bf16[1,1,2,64,1024]{4,3,2,1,0:T(8,128)(2,1)} %param.10) | copy-start | bytes 786436
  2.0 11.4 %copy-start = (bf16[1,2,4,64,1024]{4,3,2,1,0:T(8,128)(2,1)S(1)}, bf16[1,2,4,64,1024]{4,3,2,1,0:T(8,128)(2,1)}, u32[]{:S(2)}) copy-start(bf16[1,2,4,64,1024]{4,3,2,1,0:T(8,128)(2,1)} %param.6) | copy-start | bytes 3145732
  2.1 11.4 %copy-start.5 = (s32[4,8,1]{1,2,0:T(1,128)S(1)}, s32[4,8,1]{1,2,0:T(1,128)}, u32[]{:S(2)}) copy-start(s32[4,8,1]{1,2,0:T(1,128)} %param.7) | copy-start | bytes 388
  2.3 11.2 %collective-permute-start = (bf16[8,64,1024]{2,1,0:T(8,128)(2,1)S(1)}, bf16[8,64,1024]{2,1,0:T(8,128)(2,1)S(1)}, u32[]{:S(2)}, u32[]{:S(2)}) collective-permute-start(bf16[8,64,1024]{2,1,0:T(8,128)(2,1)S(1)} %pad_maximum_fusion), channel_id=1, source_target_pairs={{0,64},{64,0},{1,65},{65,1},{2,66},{66,2},{3,67},{67,3},{4,68},{68... | collective-permute-start | bytes 3145736 | tf_op jit(solution)/shard_map/ppermute | solution.py:153
  15.4 24.0 %all-to-all-start = ((bf16[4,3,64,1024]{3,2,1,0:T(8,128)(2,1)}), bf16[4,3,64,1024]{3,2,1,0:T(8,128)(2,1)S(1)}, u32[]{:S(2)}, u32[]{:S(2)}) async-start(bf16[4,3,64,1024]{3,2,1,0:T(8,128)(2,1)} %pack.1), calls=%async_computation | async-start | bytes 3145728 | tf_op jit(solution)/shard_map/all_to_all | solution.py:156
  131.8 2.0 %copy-start.3 = (f32[1,1,2,64,1024]{4,3,2,1,0:T(8,128)S(1)}, f32[1,1,2,64,1024]{4,3,2,1,0:T(8,128)}, u32[]{:S(2)}) copy-start(f32[1,1,2,64,1024]{4,3,2,1,0:T(8,128)} %param.8) | copy-start | bytes 1572868
  131.8 2.0 %copy-start.4 = (f32[1,1,2,64,1024]{4,3,2,1,0:T(8,128)S(1)}, f32[1,1,2,64,1024]{4,3,2,1,0:T(8,128)}, u32[]{:S(2)}) copy-start(f32[1,1,2,64,1024]{4,3,2,1,0:T(8,128)} %param.9) | copy-start | bytes 1572868
